TPU v7x, 512 devices: a whole 4x8x8 slice. The times are simulated.
512 devices in a mesh: rows: 16 (over x_lo, z), cols: 32 (over x_hi, y, core).
Axes of the slice: x: 4 (x_hi: 2, x_lo: 2; x = x_hi * 2 + x_lo), y: 8, z: 8, core: 2. Of those that a mesh axis runs over, the one named last changes fastest.
Arguments:
- image_embed: bfloat16 [262144, 1152], P(('rows', 'cols')), may hold values from -0.1875 to 0.1875
- text_embed: bfloat16 [262144, 1152], P(('rows', 'cols')), may hold values from -0.1875 to 0.1875
- pair_ids: int32 [262144], P(('rows', 'cols')), may hold values from 0 to 262143, as said below
- log_scale: float32 [1], replicated, may hold values from 1.6 to 3
- logit_bias: float32 [1], replicated, may hold values from -3 to -1
Outputs:
- row_loss: float32 [262144], P(('rows', 'cols'))
- grad_image: bfloat16 [262144, 1152], P(('rows', 'cols'))
- grad_text: bfloat16 [262144, 1152], P(('rows', 'cols'))
Inputs may be any that keep to these rules, and one draw needn't show every extreme that they name: `pair_ids`: positions 0 to 262143 fall in aligned groups of 1024 positions; the id of a pair lies within its own group's range of positions, so pairs of different groups never match.
All inputs are finite; a program needn't handle non-finite values.
Results may differ from a plain program's by a relative error of at most 0.005.
Values may be sent and summed in bfloat16 or wider, within the bound.
No kernel may reach another device: no remote copies, remote signals or barrier semaphores. Data moves between devices by JAX's collectives and lax.ppermute only.
A program may use at most 64 MiB of HBM per device.

v0:
```python
import jax
import jax.numpy as jnp
from jax import lax
from jax.sharding import PartitionSpec as P

STEPS = 4


def from_behind(array, axis, by):
    size = lax.axis_size(axis)
    return lax.ppermute(array, axis, [(i, (i + by) % size) for i in range(size)])


def slope_terms(image_block, text_block, own_ids, other_ids, logit_scale, shift_term):
    logits = (
        logit_scale * jnp.dot(image_block, text_block.T, preferred_element_type=jnp.float32)
        + shift_term
    )
    positive = (own_ids[:, None] == other_ids[None, :]).astype(jnp.float32)
    row_terms = jnp.sum(jax.nn.softplus(logits) - positive * logits, axis=1)
    slopes = (jax.nn.sigmoid(logits) - positive).astype(jnp.bfloat16)
    return (row_terms, slopes)


def block_terms(image_block, text_block, own_ids, other_ids, logit_scale, shift_term):
    row_terms, slopes = slope_terms(
        image_block, text_block, own_ids, other_ids, logit_scale, shift_term
    )
    image_part = jnp.dot(slopes, text_block, preferred_element_type=jnp.float32)
    text_part = jnp.dot(slopes.T, image_block, preferred_element_type=jnp.float32)
    return (row_terms, image_part, text_part)


def local(image_embed, text_embed, pair_ids, log_scale, logit_bias):
    logit_scale = jnp.exp(log_scale[0])
    shift_term = logit_bias[0]
    rows_here = image_embed.shape[0]
    loss_sum = jnp.zeros((rows_here,), jnp.float32)
    image_total = jnp.zeros(image_embed.shape, jnp.float32)
    text_total = jnp.zeros(text_embed.shape, jnp.float32)
    visiting = (text_embed, pair_ids)
    for k in range(STEPS):
        if k > 0:
            visiting = from_behind((visiting[0], visiting[1]), ("rows", "cols"), 1)
        row_terms, image_part, text_part = block_terms(
            image_embed, visiting[0], pair_ids, visiting[1], logit_scale, shift_term
        )
        loss_sum = loss_sum + row_terms
        image_total = image_total + image_part
        if k == 0:
            text_total = text_part
        else:
            text_total = text_total + from_behind(text_part, ("rows", "cols"), -k)
    row_loss = loss_sum / (STEPS * rows_here)
    grad_image = (logit_scale * image_total).astype(jnp.bfloat16)
    grad_text = (logit_scale * text_total).astype(jnp.bfloat16)
    return (row_loss, grad_image, grad_text)


def solution(mesh):
    in_specs = (P(("rows", "cols"), None), P(("rows", "cols"), None), P(("rows", "cols")), P(), P())
    out_specs = (P(("rows", "cols")), P(("rows", "cols"), None), P(("rows", "cols"), None))
    return jax.shard_map(local, mesh=mesh, in_specs=in_specs, out_specs=out_specs, check_vma=False)
```

profile of v0, /device:TPU:255, one launch (start us, length us, event | category | flops | bytes accessed | tf_op | source)
XLA Modules:
  0.0 247.4 jit_solution(17004341282635809543)
XLA Ops:
  0.6 0.0 copy-start
  0.6 6.0 %collective-permute-start = (bf16[512,1152]{1,0:T(8,128)(2,1)}, bf16[512,1152]{1,0:T(8,128)(2,1)S(1)}, u32[]{:S(2)}, u32[]{:S(2)}) collective-permute-start(bf16[512,1152]{1,0:T(8,128)(2,1)} %param.6), channel_id=1, source_target_pairs={{0,1},{1,2},{2,3},{3,4},{4,5},{5,6},{6,7},{7,8},{8,9},{9,10},{10,1... | collective-permute-start | bytes 3538952 | tf_op jit(solution)/shard_map/ppermute | solution.py:11
  6.6 13.4 %collective-permute-done = bf16[512,1152]{1,0:T(8,128)(2,1)S(1)} collective-permute-done((bf16[512,1152]{1,0:T(8,128)(2,1)}, bf16[512,1152]{1,0:T(8,128)(2,1)S(1)}, u32[]{:S(2)}, u32[]{:S(2)}) %collective-permute-start) | collective-permute-done | bytes 1179680 | tf_op jit(solution)/shard_map/ppermute | solution.py:11
  20.0 10.0 %collective-permute-start.2 = (bf16[512,1152]{1,0:T(8,128)(2,1)S(1)}, bf16[512,1152]{1,0:T(8,128)(2,1)S(1)}, u32[]{:S(2)}, u32[]{:S(2)}) collective-permute-start(bf16[512,1152]{1,0:T(8,128)(2,1)S(1)} %collective-permute-done), channel_id=1, source_target_pairs={{0,1},{1,2},{2,3},{3,4},{4,5},{5,6},{6,7},{7,8},{8,9},{9,10},{10,1... | collective-permute-start | bytes 3538952 | tf_op jit(solution)/shard_map/ppermute | solution.py:11
  30.0 13.1 %collective-permute-done.2 = bf16[512,1152]{1,0:T(8,128)(2,1)S(1)} collective-permute-done((bf16[512,1152]{1,0:T(8,128)(2,1)S(1)}, bf16[512,1152]{1,0:T(8,128)(2,1)S(1)}, u32[]{:S(2)}, u32[]{:S(2)}) %collective-permute-start.2) | collective-permute-done | bytes 1179680 | tf_op jit(solution)/shard_map/ppermute | solution.py:11
  43.2 10.1 %collective-permute-start.4 = (bf16[512,1152]{1,0:T(8,128)(2,1)S(1)}, bf16[512,1152]{1,0:T(8,128)(2,1)S(1)}, u32[]{:S(2)}, u32[]{:S(2)}) collective-permute-start(bf16[512,1152]{1,0:T(8,128)(2,1)S(1)} %collective-permute-done.2), channel_id=1, source_target_pairs={{0,1},{1,2},{2,3},{3,4},{4,5},{5,6},{6,7},{7,8},{8,9},{9,10},{10,1... | collective-permute-start | bytes 3538952 | tf_op jit(solution)/shard_map/ppermute | solution.py:11
  53.3 1.9 collective-permute-start.1
  56.5 9.9 %collective-permute-done.1 = s32[512]{0:T(512)S(1)} collective-permute-done((s32[512]{0:T(512)}, s32[512]{0:T(512)S(1)}, u32[]{:S(2)}, u32[]{:S(2)}) %collective-permute-start.1) | collective-permute-done | bytes 2080 | tf_op jit(solution)/shard_map/ppermute | solution.py:11
  66.4 10.1 %collective-permute-start.3 = (s32[512]{0:T(512)S(1)}, s32[512]{0:T(512)S(1)}, u32[]{:S(2)}, u32[]{:S(2)}) collective-permute-start(s32[512]{0:T(512)S(1)} %collective-permute-done.1), channel_id=1, source_target_pairs={{0,1},{1,2},{2,3},{3,4},{4,5},{5,6},{6,7},{7,8},{8,9},{9,10},{10,1... | collective-permute-start | bytes 6152 | tf_op jit(solution)/shard_map/ppermute | solution.py:11
  76.5 0.0 copy-done
  76.5 2.1 fusion.9
  78.7 0.0 collective-permute-done.3
  78.7 8.4 %collective-permute-start.5 = (s32[512]{0:T(512)S(1)}, s32[512]{0:T(512)S(1)}, u32[]{:S(2)}, u32[]{:S(2)}) collective-permute-start(s32[512]{0:T(512)S(1)} %collective-permute-done.3), channel_id=1, source_target_pairs={{0,1},{1,2},{2,3},{3,4},{4,5},{5,6},{6,7},{7,8},{8,9},{9,10},{10,1... | collective-permute-start | bytes 6152 | tf_op jit(solution)/shard_map/ppermute | solution.py:11
  87.2 0.0 copy-start.1
  87.2 0.9 fusion.7
  88.1 0.0 copy-done.1
  88.1 1.0 fusion.32
  89.1 1.9 collective-permute-start.7
  91.0 0.0 collective-permute-done.4
  91.0 0.9 fusion.6
  91.9 0.0 collective-permute-done.5
  91.9 1.0 fusion.29
  92.9 1.9 collective-permute-start.8
  94.9 3.3 %fusion.15 = (f32[512]{0:T(512)S(1)}, f32[512]{0:T(512)S(1)}, f32[512]{0:T(512)S(1)}, f32[512]{0:T(512)S(1)}, f32[512,512]{0,1:T(8,128)S(1)}) fusion(s32[512]{0:T(512)S(1)} %copy-done.1, s32[512]{0:T(512)S(1)} %collective-permute-done.1, f32[512,512]{0,1:T(8,128)S(1)} %fusion.7, s32[512]{0:T(512)S(1)} %collective-permute-done.3, f32[512,512]{0,1:T(8,128)S(1)} %fusion.6, ...), kind=kOutput, calls=%fused_computation.35 | convolution fusion | flops 614987776 | bytes 6569992 | tf_op jit(solution)/shard_map/dot_general | solution.py:16
  98.1 0.0 copy-start.2
  98.2 1.0 fusion.35
  99.2 2.1 collective-permute-start.6
  101.3 0.0 copy-done.2
  101.3 1.0 fusion.27
  102.3 0.6 add_multiply_fusion
  102.9 1.0 convolution_add_fusion.3
  103.8 1.0 convolution_add_fusion.2
  104.8 2.0 fusion.4
  106.8 45.5 %collective-permute-done.7 = f32[512,1152]{1,0:T(8,128)S(1)} collective-permute-done((f32[512,1152]{1,0:T(8,128)S(1)}, f32[512,1152]{1,0:T(8,128)S(1)}, u32[]{:S(2)}, u32[]{:S(2)}) %collective-permute-start.7) | collective-permute-done | bytes 2359328 | tf_op jit(solution)/shard_map/ppermute | solution.py:11
  152.3 65.7 %collective-permute-done.8 = f32[512,1152]{1,0:T(8,128)S(1)} collective-permute-done((f32[512,1152]{1,0:T(8,128)S(1)}, f32[512,1152]{1,0:T(8,128)S(1)}, u32[]{:S(2)}, u32[]{:S(2)}) %collective-permute-start.8) | collective-permute-done | bytes 2359328 | tf_op jit(solution)/shard_map/ppermute | solution.py:11
  218.0 27.3 %collective-permute-done.6 = f32[512,1152]{1,0:T(8,128)S(1)} collective-permute-done((f32[512,1152]{1,0:T(8,128)S(1)}, f32[512,1152]{1,0:T(8,128)S(1)}, u32[]{:S(2)}, u32[]{:S(2)}) %collective-permute-start.6) | collective-permute-done | bytes 2359328 | tf_op jit(solution)/shard_map/ppermute | solution.py:11
  245.2 2.2 fusion.5
Async XLA Ops:
  0.6 75.9 %copy-start = (bf16[512,1152]{1,0:T(8,128)(2,1)S(1)}, bf16[512,1152]{1,0:T(8,128)(2,1)}, u32[]{:S(2)}) copy-start(bf16[512,1152]{1,0:T(8,128)(2,1)} %param.5) | copy-start | bytes 3538948
  0.6 19.4 %collective-permute-start = (bf16[512,1152]{1,0:T(8,128)(2,1)}, bf16[512,1152]{1,0:T(8,128)(2,1)S(1)}, u32[]{:S(2)}, u32[]{:S(2)}) collective-permute-start(bf16[512,1152]{1,0:T(8,128)(2,1)} %param.6), channel_id=1, source_target_pairs={{0,1},{1,2},{2,3},{3,4},{4,5},{5,6},{6,7},{7,8},{8,9},{9,10},{10,1... | collective-permute-start | bytes 3538952 | tf_op jit(solution)/shard_map/ppermute | solution.py:11
  20.0 23.1 %collective-permute-start.2 = (bf16[512,1152]{1,0:T(8,128)(2,1)S(1)}, bf16[512,1152]{1,0:T(8,128)(2,1)S(1)}, u32[]{:S(2)}, u32[]{:S(2)}) collective-permute-start(bf16[512,1152]{1,0:T(8,128)(2,1)S(1)} %collective-permute-done), channel_id=1, source_target_pairs={{0,1},{1,2},{2,3},{3,4},{4,5},{5,6},{6,7},{7,8},{8,9},{9,10},{10,1... | collective-permute-start | bytes 3538952 | tf_op jit(solution)/shard_map/ppermute | solution.py:11
  43.2 47.8 %collective-permute-start.4 = (bf16[512,1152]{1,0:T(8,128)(2,1)S(1)}, bf16[512,1152]{1,0:T(8,128)(2,1)S(1)}, u32[]{:S(2)}, u32[]{:S(2)}) collective-permute-start(bf16[512,1152]{1,0:T(8,128)(2,1)S(1)} %collective-permute-done.2), channel_id=1, source_target_pairs={{0,1},{1,2},{2,3},{3,4},{4,5},{5,6},{6,7},{7,8},{8,9},{9,10},{10,1... | collective-permute-start | bytes 3538952 | tf_op jit(solution)/shard_map/ppermute | solution.py:11
  53.3 13.1 %collective-permute-start.1 = (s32[512]{0:T(512)}, s32[512]{0:T(512)S(1)}, u32[]{:S(2)}, u32[]{:S(2)}) collective-permute-start(s32[512]{0:T(512)} %param.7), channel_id=1, source_target_pairs={{0,1},{1,2},{2,3},{3,4},{4,5},{5,6},{6,7},{7,8},{8,9},{9,10},{10,1... | collective-permute-start | bytes 6152 | tf_op jit(solution)/shard_map/ppermute | solution.py:11
  66.4 12.3 %collective-permute-start.3 = (s32[512]{0:T(512)S(1)}, s32[512]{0:T(512)S(1)}, u32[]{:S(2)}, u32[]{:S(2)}) collective-permute-start(s32[512]{0:T(512)S(1)} %collective-permute-done.1), channel_id=1, source_target_pairs={{0,1},{1,2},{2,3},{3,4},{4,5},{5,6},{6,7},{7,8},{8,9},{9,10},{10,1... | collective-permute-start | bytes 6152 | tf_op jit(solution)/shard_map/ppermute | solution.py:11
  78.7 13.2 %collective-permute-start.5 = (s32[512]{0:T(512)S(1)}, s32[512]{0:T(512)S(1)}, u32[]{:S(2)}, u32[]{:S(2)}) collective-permute-start(s32[512]{0:T(512)S(1)} %collective-permute-done.3), channel_id=1, source_target_pairs={{0,1},{1,2},{2,3},{3,4},{4,5},{5,6},{6,7},{7,8},{8,9},{9,10},{10,1... | collective-permute-start | bytes 6152 | tf_op jit(solution)/shard_map/ppermute | solution.py:11
  87.2 0.9 copy-start.1
  89.1 63.2 %collective-permute-start.7 = (f32[512,1152]{1,0:T(8,128)S(1)}, f32[512,1152]{1,0:T(8,128)S(1)}, u32[]{:S(2)}, u32[]{:S(2)}) collective-permute-start(f32[512,1152]{1,0:T(8,128)S(1)} %fusion.32), channel_id=1, source_target_pairs={{0,510},{1,511},{2,0},{3,1},{4,2},{5,3},{6,4},{7,5},{8,6},{9,7},{1... | collective-permute-start | bytes 7077896 | tf_op jit(solution)/shard_map/ppermute | solution.py:11
  92.9 125.0 %collective-permute-start.8 = (f32[512,1152]{1,0:T(8,128)S(1)}, f32[512,1152]{1,0:T(8,128)S(1)}, u32[]{:S(2)}, u32[]{:S(2)}) collective-permute-start(f32[512,1152]{1,0:T(8,128)S(1)} %fusion.29), channel_id=1, source_target_pairs={{0,509},{1,510},{2,511},{3,0},{4,1},{5,2},{6,3},{7,4},{8,5},{9,6},... | collective-permute-start | bytes 7077896 | tf_op jit(solution)/shard_map/ppermute | solution.py:11
  98.1 3.1 %copy-start.2 = (bf16[512,1152]{1,0:T(8,128)(2,1)S(1)}, bf16[512,1152]{1,0:T(8,128)(2,1)}, u32[]{:S(2)}) copy-start(bf16[512,1152]{1,0:T(8,128)(2,1)} %param.6) | copy-start | bytes 3538948
  99.2 146.1 %collective-permute-start.6 = (f32[512,1152]{1,0:T(8,128)S(1)}, f32[512,1152]{1,0:T(8,128)S(1)}, u32[]{:S(2)}, u32[]{:S(2)}) collective-permute-start(f32[512,1152]{1,0:T(8,128)S(1)} %fusion.35), channel_id=1, source_target_pairs={{0,511},{1,0},{2,1},{3,2},{4,3},{5,4},{6,5},{7,6},{8,7},{9,8},{10,... | collective-permute-start | bytes 7077896 | tf_op jit(solution)/shard_map/ppermute | solution.py:11
where the time goes:
time: 248 us; the launch traced here: 247 us
  waiting for transfers between devices  175 us (71%)
  starting transfers between devices  52.4 us (21%)
  matrix products  17.3 us (7%)
    ppermute x9, waiting for transfers between devices, from_behind(): lax.ppermute(array, axis, [(i, (i + by) % size) for i in range(size)])  175 us
    ppermute x9, starting transfers between devices, from_behind(): lax.ppermute(array, axis, [(i, (i + by) % size) for i in range(size)])  52.4 us
    dot_general x4, matrix products, slope_terms(): jnp.dot(image_block, text_block.T, preferred_element_type=jnp.float32)  7.18 us
    dot_general x4, matrix products, block_terms(): jnp.dot(slopes.T, image_block, preferred_element_type=jnp.float32)  5.18 us
  transfers between devices with their start and end apart: 9, of which 6 were waited for; matrix products, arithmetic and copies ran while one was open for 6% of the time, Pallas kernels for 0%

commit v1 on v0

v1 whole, which is shorter than its diff:
```python
import jax
import jax.numpy as jnp
from jax import lax
from jax.sharding import PartitionSpec as P

STEPS = 4
AXES = ("rows", "cols")


def swap_in_chip(size):
    return [(i, i ^ 1) for i in range(size)]


def swap_across(size):
    return [(i, (i + 1) % size if i % 2 else (i - 1) % size) for i in range(size)]


def two_along(size):
    return [(i, (i - 2) % size if i % 2 else (i + 2) % size) for i in range(size)]


def scores(own, other, scale, shift):
    return scale * lax.dot_general(
        own, other, (((1,), (1,)), ((), ())), preferred_element_type=jnp.float32
    ) + shift


def times(slopes, other):
    return jnp.dot(slopes, other, preferred_element_type=jnp.float32)


def far_pair(own, other, scale, shift):
    logits = scores(own, other, scale, shift)
    row_terms = jnp.sum(jax.nn.softplus(logits), axis=1)
    slopes = jax.nn.sigmoid(logits).astype(jnp.bfloat16)
    return row_terms, times(slopes, other)


def near_slopes(own, other, own_ids, other_ids, scale, shift):
    logits = scores(own, other, scale, shift)
    positive = (own_ids[:, None] == other_ids[None, :]).astype(jnp.float32)
    row_terms = jnp.sum(jax.nn.softplus(logits) - positive * logits, axis=1)
    return row_terms, (jax.nn.sigmoid(logits) - positive).astype(jnp.bfloat16)


def after(array, *others):
    return lax.optimization_barrier((array,) + others)[0]


def local(image, text, ids, log_scale, logit_bias):
    scale = jnp.exp(log_scale[0])
    shift = logit_bias[0]
    rows = image.shape[0]
    size = lax.axis_size(AXES)
    even = lax.rem(lax.axis_index(AXES), 2) == 0
    ahead = jnp.where(even, image, text)
    beside = jnp.where(even, text, image)

    cross1 = lax.ppermute(ahead, AXES, swap_across(size))
    chip1 = lax.ppermute(beside, AXES, swap_in_chip(size))
    chip_ids = lax.ppermute(ids, AXES, swap_in_chip(size))

    loss, slopes = near_slopes(image, text, ids, ids, scale, shift)
    image_total = times(slopes, text)
    text_total = times(slopes.T, image)

    cross2 = lax.ppermute(after(beside, image_total, text_total), AXES, two_along(size))

    chip_loss, slopes = near_slopes(beside, chip1, ids, chip_ids, scale, shift)
    chip_total = times(slopes, chip1)

    cross3 = lax.ppermute(cross1, AXES, two_along(size))
    chip2 = lax.ppermute(cross1, AXES, swap_in_chip(size))
    cross_loss, cross_total = far_pair(ahead, cross1, scale, shift)
    more_loss, more = far_pair(beside, chip2, scale, shift)
    chip_loss, chip_total = chip_loss + more_loss, chip_total + more

    chip3 = lax.ppermute(cross2, AXES, swap_in_chip(size))
    more_loss, more = far_pair(ahead, cross2, scale, shift)
    cross_loss, cross_total = cross_loss + more_loss, cross_total + more
    more_loss, more = far_pair(beside, chip3, scale, shift)
    chip_loss, chip_total = chip_loss + more_loss, chip_total + more

    more_loss, more = far_pair(ahead, cross3, scale, shift)
    cross_loss, cross_total = cross_loss + more_loss, cross_total + more

    row_loss = (loss + jnp.where(even, cross_loss, chip_loss)) / (STEPS * rows)
    image_total = image_total + jnp.where(even, cross_total, chip_total)
    text_total = text_total + jnp.where(even, chip_total, cross_total)
    grad_image = (scale * image_total).astype(jnp.bfloat16)
    grad_text = (scale * text_total).astype(jnp.bfloat16)
    return row_loss, grad_image, grad_text


def solution(mesh):
    in_specs = (P(AXES, None), P(AXES, None), P(AXES), P(), P())
    out_specs = (P(AXES), P(AXES, None), P(AXES, None))
    return jax.shard_map(local, mesh=mesh, in_specs=in_specs, out_specs=out_specs, check_vma=False)
```

time: 248 us -> 68.6 us (0.28)
  the two profiles are of different devices: /device:TPU:255 before, /device:TPU:1 now
where the time goes in v1:
time: 68.6 us; the launch traced here: 68.2 us
  starting transfers between devices  43.3 us (63%)
  matrix products  19.3 us (28%)
  other arithmetic  2.58 us (4%)
  between operations  2.19 us (3%)
  waiting for transfers between devices  0.83 us (1%)
    ppermute x1, starting transfers between devices, local(): cross3 = lax.ppermute(cross1, AXES, two_along(size))  15 us
    ppermute x1, starting transfers between devices, local(): chip1 = lax.ppermute(beside, AXES, swap_in_chip(size))  14.3 us
    dot_general x7, matrix products, scores(): lax.dot_general(own, other, (((1,), (1,)), ((), ())), preferred_element_t...  10 us
    dot_general x8, matrix products, times(): return jnp.dot(slopes, other, preferred_element_type=jnp.float32)  9.27 us
    ppermute x1, starting transfers between devices, local(): cross1 = lax.ppermute(ahead, AXES, swap_across(size))  4.59 us
    ppermute x1, starting transfers between devices, local(): lax.ppermute(after(beside, image_total, text_total), AXES, two_along(size))  2.98 us
    ppermute x1, starting transfers between devices, local(): chip3 = lax.ppermute(cross2, AXES, swap_in_chip(size))  2.6 us
    select_n x1, other arithmetic, local(): ahead = jnp.where(even, image, text)  1.99 us
  transfers between devices with their start and end apart: 7, of which 1 were waited for; matrix products, arithmetic and copies ran while one was open for 20% of the time, Pallas kernels for 0%

profile of v1, /device:TPU:1, one launch (start us, length us, event | category | flops | bytes accessed | tf_op | source)
XLA Modules:
  0.0 68.2 jit_solution(5295949758007606983)
XLA Ops:
  0.6 0.0 copy-start
  0.6 0.0 copy-start.1
  0.7 2.0 %broadcast_select_fusion.1 = (bf16[512,1152]{1,0:T(8,128)(2,1)S(1)}, bf16[512,1152]{1,0:T(8,128)(2,1)S(1)}) fusion(bf16[512,1152]{1,0:T(8,128)(2,1)} %param.5, bf16[512,1152]{1,0:T(8,128)(2,1)} %param.6, pred[]{:T(512)S(6)} %eq.30), kind=kLoop, calls=%fused_computation.32 | loop fusion | flops 1179648 | bytes 4718593 | tf_op jit(solution)/shard_map/jit(_where)/select_n | solution.py:56
  2.7 4.6 %collective-permute-start = (bf16[512,1152]{1,0:T(8,128)(2,1)S(1)}, bf16[512,1152]{1,0:T(8,128)(2,1)S(1)}, u32[]{:S(2)}, u32[]{:S(2)}) collective-permute-start(bf16[512,1152]{1,0:T(8,128)(2,1)S(1)} %get-tuple-element.9), channel_id=1, source_target_pairs={{0,511},{1,2},{2,1},{3,4},{4,3},{5,6},{6,5},{7,8},{8,7},{9,10},{10... | collective-permute-start | bytes 3538952 | tf_op jit(solution)/shard_map/ppermute | solution.py:59
  7.3 14.3 %collective-permute-start.3 = (bf16[512,1152]{1,0:T(8,128)(2,1)S(1)}, bf16[512,1152]{1,0:T(8,128)(2,1)S(1)}, u32[]{:S(2)}, u32[]{:S(2)}) collective-permute-start(bf16[512,1152]{1,0:T(8,128)(2,1)S(1)} %get-tuple-element.4), channel_id=1, source_target_pairs={{0,1},{1,0},{2,3},{3,2},{4,5},{5,4},{6,7},{7,6},{8,9},{9,8},{10,11... | collective-permute-start | bytes 3538952 | tf_op jit(solution)/shard_map/ppermute | solution.py:60
  22.9 0.0 copy-done
  22.9 0.0 copy-done.1
  22.9 0.0 copy-start.2
  22.9 0.9 %fusion.6 = f32[512,512]{0,1:T(8,128)S(1)} fusion(bf16[512,1152]{1,0:T(8,128)(2,1)S(1)} %copy-done, bf16[512,1152]{1,0:T(8,128)(2,1)S(1)} %copy-done.1, f32[]{:T(128)} %bitcast.24, f32[]{:T(128)} %bitcast), kind=kOutput, calls=%fused_computation.26 | convolution fusion | flops 604504064 | bytes 3407880 | tf_op jit(solution)/shard_map/dot_general | solution.py:23
  23.8 0.0 copy-done.2
  23.8 1.0 %fusion.37 = f32[512,1152]{1,0:T(8,128)S(1)} fusion(bf16[512,1152]{1,0:T(8,128)(2,1)S(1)} %copy-done, f32[512,512]{0,1:T(8,128)S(1)} %fusion.6, s32[512]{0:T(512)S(1)} %copy-done.2), kind=kOutput, calls=%fused_computation.68 | convolution fusion | flops 605814784 | bytes 4589568 | tf_op jit(solution)/shard_map/dot_general | solution.py:29
  24.8 1.0 %fusion.39 = f32[512,1152]{1,0:T(8,128)S(1)} fusion(bf16[512,1152]{1,0:T(8,128)(2,1)S(1)} %copy-done.1, f32[512,512]{0,1:T(8,128)S(1)} %fusion.6, s32[512]{0:T(512)S(1)} %copy-done.2), kind=kOutput, calls=%fused_computation.69 | convolution fusion | flops 605814784 | bytes 4589568 | tf_op jit(solution)/shard_map/dot_general | solution.py:29
  25.8 3.0 %collective-permute-start.1 = (bf16[512,1152]{1,0:T(8,128)(2,1)S(1)}, bf16[512,1152]{1,0:T(8,128)(2,1)S(1)}, u32[]{:S(2)}, u32[]{:S(2)}) collective-permute-start(bf16[512,1152]{1,0:T(8,128)(2,1)S(1)} %get-tuple-element.4), channel_id=1, source_target_pairs={{0,2},{1,511},{2,4},{3,1},{4,6},{5,3},{6,8},{7,5},{8,10},{9,7},{10... | collective-permute-start | bytes 3538952 | tf_op jit(solution)/shard_map/ppermute | solution.py:67
  28.8 1.9 %collective-permute-start.4 = (s32[512]{0:T(512)S(1)}, s32[512]{0:T(512)S(1)}, u32[]{:S(2)}, u32[]{:S(2)}) collective-permute-start(s32[512]{0:T(512)S(1)} %copy-done.2), channel_id=1, source_target_pairs={{0,1},{1,0},{2,3},{3,2},{4,5},{5,4},{6,7},{7,6},{8,9},{9,8},{10,11... | collective-permute-start | bytes 6152 | tf_op jit(solution)/shard_map/ppermute | solution.py:61
  30.7 0.0 collective-permute-done
  30.8 15.0 %collective-permute-start.2 = (bf16[512,1152]{1,0:T(8,128)(2,1)S(1)}, bf16[512,1152]{1,0:T(8,128)(2,1)S(1)}, u32[]{:S(2)}, u32[]{:S(2)}) collective-permute-start(bf16[512,1152]{1,0:T(8,128)(2,1)S(1)} %collective-permute-done), channel_id=1, source_target_pairs={{0,2},{1,511},{2,4},{3,1},{4,6},{5,3},{6,8},{7,5},{8,10},{9,7},{10... | collective-permute-start | bytes 3538952 | tf_op jit(solution)/shard_map/ppermute | solution.py:72
  45.8 1.9 %collective-permute-start.5 = (bf16[512,1152]{1,0:T(8,128)(2,1)S(1)}, bf16[512,1152]{1,0:T(8,128)(2,1)S(1)}, u32[]{:S(2)}, u32[]{:S(2)}) collective-permute-start(bf16[512,1152]{1,0:T(8,128)(2,1)S(1)} %collective-permute-done), channel_id=1, source_target_pairs={{0,1},{1,0},{2,3},{3,2},{4,5},{5,4},{6,7},{7,6},{8,9},{9,8},{10,11... | collective-permute-start | bytes 3538952 | tf_op jit(solution)/shard_map/ppermute | solution.py:73
  47.7 0.0 collective-permute-done.4
  47.7 0.0 collective-permute-done.3
  47.7 2.1 %fusion.12 = (f32[512]{0:T(512)S(1)}, f32[512]{0:T(512)S(1)}, f32[512,512]{0,1:T(8,128)S(1)}) fusion(s32[512]{0:T(512)S(1)} %copy-done.2, s32[512]{0:T(512)S(1)} %collective-permute-done.4, f32[512,512]{0,1:T(8,128)S(1)} %fusion.6, f32[]{:T(128)} %bitcast.27, bf16[512,1152]{1,0:T(8,128)(2,1)S(1)} %get-tuple-element.4, ...), kind=kOutput, calls=%fused_computation.38 | convolution fusion | flops 609745920 | bytes 4464648 | tf_op jit(solution)/shard_map/dot_general | solution.py:23
  49.8 1.0 %fusion.20 = f32[512,1152]{1,0:T(8,128)S(1)} fusion(bf16[512,1152]{1,0:T(8,128)(2,1)S(1)} %collective-permute-done.3, f32[512,512]{0,1:T(8,128)S(1)} %get-tuple-element.11, s32[512]{0:T(512)S(1)} %copy-done.2, s32[512]{0:T(512)S(1)} %collective-permute-done.4), kind=kOutput, calls=%fused_computation.51 | convolution fusion | flops 605814784 | bytes 4591616 | tf_op jit(solution)/shard_map/dot_general | solution.py:29
  50.8 0.0 collective-permute-done.1
  50.8 2.6 %collective-permute-start.6 = (bf16[512,1152]{1,0:T(8,128)(2,1)S(1)}, bf16[512,1152]{1,0:T(8,128)(2,1)S(1)}, u32[]{:S(2)}, u32[]{:S(2)}) collective-permute-start(bf16[512,1152]{1,0:T(8,128)(2,1)S(1)} %collective-permute-done.1), channel_id=1, source_target_pairs={{0,1},{1,0},{2,3},{3,2},{4,5},{5,4},{6,7},{7,6},{8,9},{9,8},{10,11... | collective-permute-start | bytes 3538952 | tf_op jit(solution)/shard_map/ppermute | solution.py:78
  53.4 1.4 %fusion.16 = (f32[512]{0:T(512)S(1)}, f32[512,512]{0,1:T(8,128)S(1)}) fusion(f32[]{:T(128)} %bitcast.29, bf16[512,1152]{1,0:T(8,128)(2,1)S(1)} %get-tuple-element.9, bf16[512,1152]{1,0:T(8,128)(2,1)S(1)} %collective-permute-done.1, f32[]{:T(128)} %bitcast), kind=kOutput, calls=%fused_computation.42 | convolution fusion | flops 606338560 | bytes 3409928 | tf_op jit(solution)/shard_map/dot_general | solution.py:23
  54.9 0.9 %fusion.22 = f32[512,1152]{1,0:T(8,128)S(1)} fusion(bf16[512,1152]{1,0:T(8,128)(2,1)S(1)} %collective-permute-done.1, f32[512,512]{0,1:T(8,128)S(1)} %get-tuple-element.21), kind=kOutput, calls=%fused_computation.52 | convolution fusion | flops 605028352 | bytes 4587520 | tf_op jit(solution)/shard_map/dot_general | solution.py:29
  55.8 1.4 %fusion.15 = (f32[512]{0:T(512)S(1)}, f32[512,512]{0,1:T(8,128)S(1)}) fusion(f32[]{:T(128)} %bitcast.30, bf16[512,1152]{1,0:T(8,128)(2,1)S(1)} %get-tuple-element.9, bf16[512,1152]{1,0:T(8,128)(2,1)S(1)} %collective-permute-done, f32[]{:T(128)} %bitcast), kind=kOutput, calls=%fused_computation.41 | convolution fusion | flops 606338560 | bytes 3409928 | tf_op jit(solution)/shard_map/dot_general | solution.py:23
  57.2 0.9 %convolution_add_fusion.3 = f32[512,1152]{1,0:T(8,128)S(1)} fusion(f32[512,1152]{1,0:T(8,128)S(1)} %fusion.22, bf16[512,1152]{1,0:T(8,128)(2,1)S(1)} %collective-permute-done, f32[512,512]{0,1:T(8,128)S(1)} %get-tuple-element.19), kind=kOutput, calls=%fused_computation.3 | convolution fusion | flops 605618176 | bytes 6946816 | tf_op jit(solution)/shard_map/dot_general | solution.py:29
  58.1 0.8 %collective-permute-done.2 = bf16[512,1152]{1,0:T(8,128)(2,1)S(1)} collective-permute-done((bf16[512,1152]{1,0:T(8,128)(2,1)S(1)}, bf16[512,1152]{1,0:T(8,128)(2,1)S(1)}, u32[]{:S(2)}, u32[]{:S(2)}) %collective-permute-start.2) | collective-permute-done | bytes 1179680 | tf_op jit(solution)/shard_map/ppermute | solution.py:72
  58.9 1.4 %fusion.17 = (f32[512]{0:T(512)S(1)}, f32[512,512]{0,1:T(8,128)S(1)}) fusion(f32[]{:T(128)} %bitcast.28, bf16[512,1152]{1,0:T(8,128)(2,1)S(1)} %get-tuple-element.9, bf16[512,1152]{1,0:T(8,128)(2,1)S(1)} %collective-permute-done.2, f32[]{:T(128)} %bitcast), kind=kOutput, calls=%fused_computation.43 | convolution fusion | flops 606338560 | bytes 3409928 | tf_op jit(solution)/shard_map/dot_general | solution.py:23
  60.3 0.0 collective-permute-done.5
  60.3 1.4 %fusion.18 = (f32[512]{0:T(512)S(1)}, f32[512,512]{0,1:T(8,128)S(1)}) fusion(f32[]{:T(128)} %bitcast.26, bf16[512,1152]{1,0:T(8,128)(2,1)S(1)} %get-tuple-element.4, bf16[512,1152]{1,0:T(8,128)(2,1)S(1)} %collective-permute-done.5, f32[]{:T(128)} %bitcast), kind=kOutput, calls=%fused_computation.44 | convolution fusion | flops 606338560 | bytes 3409928 | tf_op jit(solution)/shard_map/dot_general | solution.py:23
  61.7 0.0 collective-permute-done.6
  61.8 1.4 %fusion.19 = (f32[512]{0:T(512)S(1)}, f32[512,512]{0,1:T(8,128)S(1)}) fusion(f32[]{:T(128)} %bitcast.25, bf16[512,1152]{1,0:T(8,128)(2,1)S(1)} %get-tuple-element.4, bf16[512,1152]{1,0:T(8,128)(2,1)S(1)} %collective-permute-done.6, f32[]{:T(128)} %bitcast), kind=kOutput, calls=%fused_computation.45 | convolution fusion | flops 606338560 | bytes 3409928 | tf_op jit(solution)/shard_map/dot_general | solution.py:23
  63.2 0.6 add_multiply_fusion
  63.8 0.9 %convolution_add_fusion.2 = f32[512,1152]{1,0:T(8,128)S(1)} fusion(f32[512,1152]{1,0:T(8,128)S(1)} %convolution_add_fusion.3, bf16[512,1152]{1,0:T(8,128)(2,1)S(1)} %collective-permute-done.2, f32[512,512]{0,1:T(8,128)S(1)} %get-tuple-element.17), kind=kOutput, calls=%fused_computation.2 | convolution fusion | flops 605618176 | bytes 6946816 | tf_op jit(solution)/shard_map/dot_general | solution.py:29
  64.7 0.9 %convolution_add_fusion.1 = f32[512,1152]{1,0:T(8,128)S(1)} fusion(f32[512,1152]{1,0:T(8,128)S(1)} %fusion.20, bf16[512,1152]{1,0:T(8,128)(2,1)S(1)} %collective-permute-done.5, f32[512,512]{0,1:T(8,128)S(1)} %get-tuple-element.15), kind=kOutput, calls=%fused_computation.1 | convolution fusion | flops 605618176 | bytes 6946816 | tf_op jit(solution)/shard_map/dot_general | solution.py:29
  65.6 2.6 %multiply_convert_fusion = (bf16[512,1152]{1,0:T(8,128)(2,1)}, bf16[512,1152]{1,0:T(8,128)(2,1)}) fusion(f32[512,1152]{1,0:T(8,128)S(1)} %fusion.37, f32[512,1152]{1,0:T(8,128)S(1)} %convolution_add_fusion.2, f32[]{:T(128)} %bitcast, pred[]{:T(512)S(6)} %eq.30, f32[512,1152]{1,0:T(8,128)S(1)} %fusion.39, f32[512,1152]{1,0:T(8,128)S(1)} %convolution_add_fusion.1, ...), kind=kOutput, calls=%fused_computation.11 | convolution fusion | flops 610336768 | bytes 14024709 | tf_op jit(solution)/shard_map/dot_general | solution.py:29
Async XLA Ops:
  0.6 22.3 %copy-start = (bf16[512,1152]{1,0:T(8,128)(2,1)S(1)}, bf16[512,1152]{1,0:T(8,128)(2,1)}, u32[]{:S(2)}) copy-start(bf16[512,1152]{1,0:T(8,128)(2,1)} %param.5) | copy-start | bytes 3538948
  0.6 22.3 %copy-start.1 = (bf16[512,1152]{1,0:T(8,128)(2,1)S(1)}, bf16[512,1152]{1,0:T(8,128)(2,1)}, u32[]{:S(2)}) copy-start(bf16[512,1152]{1,0:T(8,128)(2,1)} %param.6) | copy-start | bytes 3538948
  2.7 28.1 %collective-permute-start = (bf16[512,1152]{1,0:T(8,128)(2,1)S(1)}, bf16[512,1152]{1,0:T(8,128)(2,1)S(1)}, u32[]{:S(2)}, u32[]{:S(2)}) collective-permute-start(bf16[512,1152]{1,0:T(8,128)(2,1)S(1)} %get-tuple-element.9), channel_id=1, source_target_pairs={{0,511},{1,2},{2,1},{3,4},{4,3},{5,6},{6,5},{7,8},{8,7},{9,10},{10... | collective-permute-start | bytes 3538952 | tf_op jit(solution)/shard_map/ppermute | solution.py:59
  7.3 40.5 %collective-permute-start.3 = (bf16[512,1152]{1,0:T(8,128)(2,1)S(1)}, bf16[512,1152]{1,0:T(8,128)(2,1)S(1)}, u32[]{:S(2)}, u32[]{:S(2)}) collective-permute-start(bf16[512,1152]{1,0:T(8,128)(2,1)S(1)} %get-tuple-element.4), channel_id=1, source_target_pairs={{0,1},{1,0},{2,3},{3,2},{4,5},{5,4},{6,7},{7,6},{8,9},{9,8},{10,11... | collective-permute-start | bytes 3538952 | tf_op jit(solution)/shard_map/ppermute | solution.py:60
  22.9 0.9 %copy-start.2 = (s32[512]{0:T(512)S(1)}, s32[512]{0:T(512)}, u32[]{:S(2)}) copy-start(s32[512]{0:T(512)} %param.7) | copy-start | bytes 6148
  25.8 25.0 %collective-permute-start.1 = (bf16[512,1152]{1,0:T(8,128)(2,1)S(1)}, bf16[512,1152]{1,0:T(8,128)(2,1)S(1)}, u32[]{:S(2)}, u32[]{:S(2)}) collective-permute-start(bf16[512,1152]{1,0:T(8,128)(2,1)S(1)} %get-tuple-element.4), channel_id=1, source_target_pairs={{0,2},{1,511},{2,4},{3,1},{4,6},{5,3},{6,8},{7,5},{8,10},{9,7},{10... | collective-permute-start | bytes 3538952 | tf_op jit(solution)/shard_map/ppermute | solution.py:67
  28.8 18.9 %collective-permute-start.4 = (s32[512]{0:T(512)S(1)}, s32[512]{0:T(512)S(1)}, u32[]{:S(2)}, u32[]{:S(2)}) collective-permute-start(s32[512]{0:T(512)S(1)} %copy-done.2), channel_id=1, source_target_pairs={{0,1},{1,0},{2,3},{3,2},{4,5},{5,4},{6,7},{7,6},{8,9},{9,8},{10,11... | collective-permute-start | bytes 6152 | tf_op jit(solution)/shard_map/ppermute | solution.py:61
  30.8 28.2 %collective-permute-start.2 = (bf16[512,1152]{1,0:T(8,128)(2,1)S(1)}, bf16[512,1152]{1,0:T(8,128)(2,1)S(1)}, u32[]{:S(2)}, u32[]{:S(2)}) collective-permute-start(bf16[512,1152]{1,0:T(8,128)(2,1)S(1)} %collective-permute-done), channel_id=1, source_target_pairs={{0,2},{1,511},{2,4},{3,1},{4,6},{5,3},{6,8},{7,5},{8,10},{9,7},{10... | collective-permute-start | bytes 3538952 | tf_op jit(solution)/shard_map/ppermute | solution.py:72
  45.8 14.5 %collective-permute-start.5 = (bf16[512,1152]{1,0:T(8,128)(2,1)S(1)}, bf16[512,1152]{1,0:T(8,128)(2,1)S(1)}, u32[]{:S(2)}, u32[]{:S(2)}) collective-permute-start(bf16[512,1152]{1,0:T(8,128)(2,1)S(1)} %collective-permute-done), channel_id=1, source_target_pairs={{0,1},{1,0},{2,3},{3,2},{4,5},{5,4},{6,7},{7,6},{8,9},{9,8},{10,11... | collective-permute-start | bytes 3538952 | tf_op jit(solution)/shard_map/ppermute | solution.py:73
  50.8 10.9 %collective-permute-start.6 = (bf16[512,1152]{1,0:T(8,128)(2,1)S(1)}, bf16[512,1152]{1,0:T(8,128)(2,1)S(1)}, u32[]{:S(2)}, u32[]{:S(2)}) collective-permute-start(bf16[512,1152]{1,0:T(8,128)(2,1)S(1)} %collective-permute-done.1), channel_id=1, source_target_pairs={{0,1},{1,0},{2,3},{3,2},{4,5},{5,4},{6,7},{7,6},{8,9},{9,8},{10,11... | collective-permute-start | bytes 3538952 | tf_op jit(solution)/shard_map/ppermute | solution.py:78

commit v2 on v1

v2 whole, which is shorter than its diff:
```python
import functools

import jax
import jax.numpy as jnp
from jax import lax
from jax.experimental import pallas as pl
from jax.experimental.pallas import tpu as pltpu
from jax.sharding import PartitionSpec as P

STEPS = 4
AXES = ("rows", "cols")
LANES = 128
COLUMNS = 256
VMEM_LIMIT = 24 * 1024 * 1024


def swap_in_chip(size):
    return [(i, i ^ 1) for i in range(size)]


def swap_across(size):
    return [(i, (i + 1) % size if i % 2 else (i - 1) % size) for i in range(size)]


def two_along(size):
    return [(i, (i - 2) % size if i % 2 else (i + 2) % size) for i in range(size)]


def after(array, *others):
    return lax.optimization_barrier((array,) + others)[0]


def is_even():
    return lax.rem(lax.axis_index("cols"), 2) == 0


def product(left, right, over_left, over_right):
    return lax.dot_general(
        left, right, (((over_left,), (over_right,)), ((), ())), preferred_element_type=jnp.float32
    )


def scale_of(log_scale_ref):
    return jnp.exp(jnp.full((1, LANES), log_scale_ref[0], jnp.float32))[:, :1]


def fold(terms):
    total = terms[:, :LANES]
    for at in range(LANES, terms.shape[1], LANES):
        total = total + terms[:, at : at + LANES]
    return total


def terms_and_slopes(logits, positive=None):
    small = jnp.exp(-jnp.abs(logits))
    terms = jnp.maximum(logits, 0.0) + jnp.log1p(small)
    slopes = jnp.where(logits >= 0, 1.0, small) / (1.0 + small)
    if positive is not None:
        terms = terms - jnp.where(positive, logits, 0.0)
        slopes = slopes - jnp.where(positive, 1.0, 0.0)
    return terms, slopes.astype(jnp.bfloat16)


def place_kernel(even_ref, odd_ref, out_ref, sem):
    def copy(ref):
        moved = pltpu.make_async_copy(ref, out_ref, sem)
        moved.start()
        moved.wait()

    even = is_even()

    @pl.when(even)
    def _():
        copy(even_ref)

    @pl.when(jnp.logical_not(even))
    def _():
        copy(odd_ref)


def ids_down(ids_ref):
    ids = ids_ref[...]
    return jnp.broadcast_to(ids, (LANES, ids.shape[1])).T


def match(down, ids_ref, columns):
    parts = [
        down == ids_ref[:, at : at + LANES]
        for at in range(columns.start, columns.stop, LANES)
    ]
    return jnp.concatenate(parts, axis=1)


def own_kernel(image_ref, text_ref, ids_ref, log_scale_ref, bias_ref, ahead_ref, beside_ref, loss_ref, slopes_ref):
    scale, shift = scale_of(log_scale_ref), bias_ref[0]
    down = ids_down(ids_ref)
    rows = image_ref.shape[0]
    for at in range(0, rows, COLUMNS):
        columns = slice(at, at + COLUMNS)
        logits = scale * product(image_ref[...], text_ref[columns, :], 1, 1) + shift
        terms, slopes = terms_and_slopes(logits, match(down, ids_ref, columns))
        slopes_ref[:, columns] = slopes
        loss_ref[...] = fold(terms) if at == 0 else loss_ref[...] + fold(terms)

    def parts(image_total, text_total):
        image_total[...] = product(slopes_ref[...], text_ref[...], 1, 0)
        text_total[...] = product(slopes_ref[...], image_ref[...], 0, 0)

    even = is_even()

    @pl.when(even)
    def _():
        parts(ahead_ref, beside_ref)

    @pl.when(jnp.logical_not(even))
    def _():
        parts(beside_ref, ahead_ref)


def pair(own_ref, other_ref, log_scale_ref, bias_ref, total_in, loss_in, total_ref, loss_ref, image_if_even, ids=None):
    scale, shift = scale_of(log_scale_ref), bias_ref[0]
    counted = jnp.where(is_even() == image_if_even, 1.0, 0.0)
    rows = own_ref.shape[0]
    down = None if ids is None else ids_down(ids[0])
    for at in range(0, rows, COLUMNS):
        columns = slice(at, at + COLUMNS)
        logits = scale * product(own_ref[...], other_ref[columns, :], 1, 1) + shift
        positive = None if ids is None else match(down, ids[1], columns)
        terms, slopes = terms_and_slopes(logits, positive)
        first = at == 0
        loss_ref[...] = (loss_in if first else loss_ref)[...] + counted * fold(terms)
        total_ref[...] = (total_in if first else total_ref)[...] + product(slopes, other_ref[columns, :], 1, 0)


def near_kernel(own_ref, other_ref, ids_ref, other_ids_ref, log_scale_ref, bias_ref, total_in, loss_in, total_ref, loss_ref):
    pair(own_ref, other_ref, log_scale_ref, bias_ref, total_in, loss_in, total_ref, loss_ref, False, (ids_ref, other_ids_ref))


def far_kernel(image_if_even, own_ref, other_ref, log_scale_ref, bias_ref, total_in, loss_in, total_ref, loss_ref):
    pair(own_ref, other_ref, log_scale_ref, bias_ref, total_in, loss_in, total_ref, loss_ref, image_if_even)


def write_out(total, log_scale_ref, rounded_ref, sem, first_ref, second_ref):
    rounded_ref[...] = (scale_of(log_scale_ref) * total[...]).astype(jnp.bfloat16)

    def copy(ref):
        moved = pltpu.make_async_copy(rounded_ref, ref, sem)
        moved.start()
        moved.wait()

    even = is_even()

    @pl.when(even)
    def _():
        copy(first_ref)

    @pl.when(jnp.logical_not(even))
    def _():
        copy(second_ref)


def beside_kernel(own_ref, other_ref, log_scale_ref, bias_ref, total_in, loss_in, loss_ref, image_ref, text_ref, total_ref, rounded_ref, sem):
    pair(own_ref, other_ref, log_scale_ref, bias_ref, total_in, loss_in, total_ref, loss_ref, False)
    write_out(total_ref, log_scale_ref, rounded_ref, sem, text_ref, image_ref)


def ahead_kernel(own_ref, other_ref, log_scale_ref, bias_ref, total_in, loss_in, image_in, text_in, row_loss_ref, image_ref, text_ref, total_ref, loss_ref, rounded_ref, sem):
    del image_in, text_in
    pair(own_ref, other_ref, log_scale_ref, bias_ref, total_in, loss_in, total_ref, loss_ref, True)
    rows = own_ref.shape[0]
    row_loss_ref[...] = jnp.sum(loss_ref[...].T, axis=0, keepdims=True) / (STEPS * rows)
    write_out(total_ref, log_scale_ref, rounded_ref, sem, image_ref, text_ref)


def call(kernel, out_shape, in_specs, out_specs, scratch=(), aliases=None, flops=0, moved=0, exps=0):
    return pl.pallas_call(
        kernel,
        out_shape=out_shape,
        in_specs=in_specs,
        out_specs=out_specs,
        scratch_shapes=scratch,
        input_output_aliases=aliases or {},
        cost_estimate=pl.CostEstimate(flops=flops, bytes_accessed=moved, transcendentals=exps),
        compiler_params=pltpu.CompilerParams(vmem_limit_bytes=VMEM_LIMIT),
    )


def near(array):
    return pltpu.with_memory_space_constraint(array, pltpu.VMEM)


def local(image, text, ids, log_scale, logit_bias):
    size = lax.axis_size(AXES)
    rows, width = image.shape
    in_vmem = pl.BlockSpec(memory_space=pltpu.VMEM)
    in_smem = pl.BlockSpec(memory_space=pltpu.SMEM)
    anywhere = pl.BlockSpec(memory_space=pl.ANY)
    total_shape = pltpu.VMEM((rows, width), jnp.float32)
    loss_shape = pltpu.VMEM((rows, LANES), jnp.float32)
    block_shape = pltpu.VMEM((rows, width), jnp.bfloat16)
    grad_shape = jax.ShapeDtypeStruct((rows, width), jnp.bfloat16)
    flops = 2 * rows * rows * width
    costs = dict(flops=2 * flops, exps=3 * rows * rows)

    place = call(place_kernel, block_shape, [anywhere] * 2, in_vmem, [pltpu.SemaphoreType.DMA], moved=2 * rows * width * 2)
    ahead = place(image, text)
    cross1 = lax.ppermute(ahead, AXES, swap_across(size))
    beside = place(text, after(image, ahead))
    chip1 = lax.ppermute(beside, AXES, swap_in_chip(size))
    chip_ids = lax.ppermute(ids, AXES, swap_in_chip(size))

    ids, chip_ids = ids.reshape(1, rows), chip_ids.reshape(1, rows)
    ahead_total, beside_total, loss = call(
        own_kernel,
        (total_shape, total_shape, loss_shape),
        [in_vmem] * 3 + [in_smem] * 2,
        (in_vmem, in_vmem, in_vmem),
        [pltpu.VMEM((rows, rows), jnp.bfloat16)],
        flops=3 * flops,
        exps=3 * rows * rows,
    )(image, text, ids, log_scale, logit_bias)

    chain = dict(aliases={4: 0, 5: 1}, **costs)
    far_specs = [in_vmem] * 2 + [in_smem] * 2 + [in_vmem] * 2

    def far(image_if_even, own, other, total, loss):
        return call(
            functools.partial(far_kernel, image_if_even), (total_shape, loss_shape), far_specs, (in_vmem, in_vmem), **chain
        )(near(own), near(other), log_scale, logit_bias, near(total), near(loss))

    beside_total, loss = call(
        near_kernel,
        (total_shape, loss_shape),
        [in_vmem] * 4 + [in_smem] * 2 + [in_vmem] * 2,
        (in_vmem, in_vmem),
        aliases={6: 0, 7: 1},
        **costs,
    )(near(beside), near(chip1), ids, chip_ids, log_scale, logit_bias, near(beside_total), near(loss))

    cross2 = lax.ppermute(after(beside, loss), AXES, two_along(size))
    cross3 = lax.ppermute(cross1, AXES, two_along(size))
    chip2 = lax.ppermute(cross1, AXES, swap_in_chip(size))
    ahead_total, loss = far(True, ahead, cross1, ahead_total, loss)
    beside_total, loss = far(False, beside, chip2, beside_total, loss)

    chip3 = lax.ppermute(cross2, AXES, swap_in_chip(size))
    ahead_total, loss = far(True, ahead, cross2, ahead_total, loss)
    loss, grad_image, grad_text = call(
        beside_kernel,
        (loss_shape, grad_shape, grad_shape),
        far_specs,
        (in_vmem, anywhere, anywhere),
        [pltpu.VMEM((rows, width), jnp.float32), pltpu.VMEM((rows, width), jnp.bfloat16), pltpu.SemaphoreType.DMA],
        aliases={5: 0},
        **costs,
    )(near(beside), near(chip3), log_scale, logit_bias, near(beside_total), near(loss))

    row_loss, grad_image, grad_text = call(
        ahead_kernel,
        (jax.ShapeDtypeStruct((1, rows), jnp.float32), grad_shape, grad_shape),
        far_specs + [anywhere] * 2,
        (in_vmem, anywhere, anywhere),
        [
            pltpu.VMEM((rows, width), jnp.float32),
            pltpu.VMEM((rows, LANES), jnp.float32),
            pltpu.VMEM((rows, width), jnp.bfloat16),
            pltpu.SemaphoreType.DMA,
        ],
        aliases={6: 1, 7: 2},
        **costs,
    )(near(ahead), near(cross3), log_scale, logit_bias, near(ahead_total), near(loss), grad_image, grad_text)
    return row_loss.reshape(rows), grad_image, grad_text


def solution(mesh):
    in_specs = (P(AXES, None), P(AXES, None), P(AXES), P(), P())
    out_specs = (P(AXES), P(AXES, None), P(AXES, None))
    return jax.shard_map(local, mesh=mesh, in_specs=in_specs, out_specs=out_specs, check_vma=False)
```

time: 68.6 us -> 81.5 us (1.19); the launches traced: 68.2 us -> 80.1 us
  Pallas kernels: 0 us -> 24 us
  matrix products: 19.3 us -> 0 us
  waiting for transfers between devices: 0.83 us -> 13.1 us
  starting transfers between devices: 43.3 us -> 38.2 us
  other arithmetic: 2.58 us -> 0 us
  local copies, waits for them, and re-layouts: 0.01 us -> 2.54 us
    pallas_call x0 -> x9, Pallas kernels: none -> 24 us  [the longest x3 8.92 us: far(): call(functools.partial(far_kernel, image_if_even), (total_shape, loss_sha...]
    dot_general x15 -> x0, matrix products: 19.3 us -> none  [the longest x7 10 us: scores(): lax.dot_general(own, other, (((1,), (1,)), ((), ())), preferred_element_t...]
    ppermute x1, starting transfers between devices: 15 us -> 2.27 us  [local(): cross3 = lax.ppermute(cross1, AXES, two_along(size))]
    ppermute x1, waiting for transfers between devices: 0.01 us -> 11 us  [local(): cross2 = lax.ppermute(after(beside, loss), AXES, two_along(size))]
    ppermute x1, starting transfers between devices: 1.92 us -> 10.8 us  [local(): chip_ids = lax.ppermute(ids, AXES, swap_in_chip(size))]
    ppermute x1, starting transfers between devices: 2.6 us -> 8.2 us  [local(): chip3 = lax.ppermute(cross2, AXES, swap_in_chip(size))]
    ppermute x1, starting transfers between devices: 14.3 us -> 8.79 us  [local(): chip1 = lax.ppermute(beside, AXES, swap_in_chip(size))]
    ppermute x1, starting transfers between devices: 4.59 us -> 1.92 us  [local(): cross1 = lax.ppermute(ahead, AXES, swap_across(size))]
  transfers between devices with their start and end apart: 7 -> 7, of which waited for: 1 -> 2; matrix products, arithmetic and copies ran while one was open for 20% -> 0% of each run, Pallas kernels for 0% -> 24%
where the time goes in v2:
time: 81.5 us; the launch traced here: 80.1 us
  starting transfers between devices  38.2 us (47%)
  Pallas kernels  24 us (29%)
  waiting for transfers between devices  13.1 us (16%)
  local copies, waits for them, and re-layouts  2.54 us (3%)
  between operations  2.26 us (3%)
    ppermute x1, waiting for transfers between devices, local(): cross2 = lax.ppermute(after(beside, loss), AXES, two_along(size))  11 us
    ppermute x1, starting transfers between devices, local(): chip_ids = lax.ppermute(ids, AXES, swap_in_chip(size))  10.8 us
    pallas_call x3, Pallas kernels, far(): call(functools.partial(far_kernel, image_if_even), (total_shape, loss_sha...  8.92 us
    ppermute x1, starting transfers between devices, local(): chip1 = lax.ppermute(beside, AXES, swap_in_chip(size))  8.79 us
    ppermute x1, starting transfers between devices, local(): chip3 = lax.ppermute(cross2, AXES, swap_in_chip(size))  8.2 us
    pallas_call x1, Pallas kernels, local(): call(ahead_kernel, (jax.ShapeDtypeStruct((1, rows), jnp.float32), grad_sh...  4.32 us
    pallas_call x1, Pallas kernels, local(): call(beside_kernel, (loss_shape, grad_shape, grad_shape), far_specs, (in_...  3.89 us
    ppermute x1, starting transfers between devices, local(): chip2 = lax.ppermute(cross1, AXES, swap_in_chip(size))  3.23 us
  transfers between devices with their start and end apart: 7, of which 2 were waited for; matrix products, arithmetic and copies ran while one was open for 0% of the time, Pallas kernels for 24%

profile of v2, /device:TPU:1, one launch (start us, length us, event | category | flops | bytes accessed | tf_op | source)
XLA Modules:
  0.0 80.1 jit_solution(10131594016406907913)
XLA Ops:
  0.6 0.0 copy-start
  0.6 1.3 %copy-done = bf16[512,1152]{1,0:T(8,128)(2,1)S(1)} copy-done((bf16[512,1152]{1,0:T(8,128)(2,1)S(1)}, bf16[512,1152]{1,0:T(8,128)(2,1)}, u32[]{:S(2)}) %copy-start) | copy-done | bytes 1179672
  1.9 0.0 copy-start.1
  1.9 1.3 %copy-done.1 = bf16[512,1152]{1,0:T(8,128)(2,1)S(1)} copy-done((bf16[512,1152]{1,0:T(8,128)(2,1)S(1)}, bf16[512,1152]{1,0:T(8,128)(2,1)}, u32[]{:S(2)}) %copy-start.1) | copy-done | bytes 1179672
  3.2 0.2 shard_map.76.own_ref
  3.4 0.0 copy-start.2
  3.4 0.3 shard_map.77.own_ref
  3.7 8.8 %collective-permute-start.2 = (bf16[512,1152]{1,0:T(8,128)(2,1)S(1)}, bf16[512,1152]{1,0:T(8,128)(2,1)S(1)}, u32[]{:S(2)}, u32[]{:S(2)}) collective-permute-start(bf16[512,1152]{1,0:T(8,128)(2,1)S(1)} %shard_map.77.own_ref), channel_id=1, source_target_pairs={{0,1},{1,0},{2,3},{3,2},{4,5},{5,4},{6,7},{7,6},{8,9},{9,8},{10,11... | collective-permute-start | bytes 3538952 | tf_op jit(solution)/shard_map/ppermute | solution.py:209
  12.5 1.9 %collective-permute-start = (bf16[512,1152]{1,0:T(8,128)(2,1)S(1)}, bf16[512,1152]{1,0:T(8,128)(2,1)S(1)}, u32[]{:S(2)}, u32[]{:S(2)}) collective-permute-start(bf16[512,1152]{1,0:T(8,128)(2,1)S(1)} %shard_map.76.own_ref), channel_id=1, source_target_pairs={{0,511},{1,2},{2,1},{3,4},{4,3},{5,6},{6,5},{7,8},{8,7},{9,10},{10... | collective-permute-start | bytes 3538952 | tf_op jit(solution)/shard_map/ppermute | solution.py:207
  14.4 0.0 copy-done.2
  14.5 10.8 %collective-permute-start.3 = (s32[512]{0:T(512)S(1)}, s32[512]{0:T(512)S(1)}, u32[]{:S(2)}, u32[]{:S(2)}) collective-permute-start(s32[512]{0:T(512)S(1)} %copy-done.2), channel_id=1, source_target_pairs={{0,1},{1,0},{2,3},{3,2},{4,5},{5,4},{6,7},{7,6},{8,9},{9,8},{10,11... | collective-permute-start | bytes 6152 | tf_op jit(solution)/shard_map/ppermute | solution.py:210
  26.5 3.2 %shard_map.78 = (f32[512,1152]{1,0:T(8,128)S(1)}, f32[512,1152]{1,0:T(8,128)S(1)}, f32[512,128]{1,0:T(8,128)S(1)}) custom-call(bf16[512,1152]{1,0:T(8,128)(2,1)S(1)} %copy-done, bf16[512,1152]{1,0:T(8,128)(2,1)S(1)} %copy-done.1, s32[1,512]{1,0:T(1,128)S(1)} %bitcast.3, f32[1]{0:T(128)S(6)} %copy.30.log_scale_ref, f32[1]{0:T(128)S(6)} %copy.31.bias_ref), custom_call_target="tpu_custom_call" | custom-call | flops 1811939328 | tf_op jit(solution)/shard_map/pallas_call | solution.py:213
  29.7 0.0 collective-permute-done.3
  29.7 0.0 collective-permute-done.2.other_ref
  29.8 3.1 %shard_map.79 = (f32[512,1152]{1,0:T(8,128)S(1)}, f32[512,128]{1,0:T(8,128)S(1)}) custom-call(bf16[512,1152]{1,0:T(8,128)(2,1)S(1)} %shard_map.77.own_ref, bf16[512,1152]{1,0:T(8,128)(2,1)S(1)} %collective-permute-done.2.other_ref, s32[1,512]{1,0:T(1,128)S(1)} %bitcast.4, s32[1,512]{1,0:T(1,128)S(1)} %bitcast.5, ...), custom_call_target="tpu_custom_call", output_to_operand_aliasing={{0}: (6, {}), {1}: (7, {})} | custom-call | flops 1207959552 | tf_op jit(solution)/shard_map/pallas_call | solution.py:231
  32.9 3.0 %collective-permute-start.4 = (bf16[512,1152]{1,0:T(8,128)(2,1)S(1)}, bf16[512,1152]{1,0:T(8,128)(2,1)S(1)}, u32[]{:S(2)}, u32[]{:S(2)}) collective-permute-start(bf16[512,1152]{1,0:T(8,128)(2,1)S(1)} %shard_map.77.own_ref), channel_id=1, source_target_pairs={{0,2},{1,511},{2,4},{3,1},{4,6},{5,3},{6,8},{7,5},{8,10},{9,7},{10... | collective-permute-start | bytes 3538952 | tf_op jit(solution)/shard_map/ppermute | solution.py:240
  35.9 0.0 collective-permute-done.other_ref
  35.9 3.2 %collective-permute-start.5 = (bf16[512,1152]{1,0:T(8,128)(2,1)S(1)}, bf16[512,1152]{1,0:T(8,128)(2,1)S(1)}, u32[]{:S(2)}, u32[]{:S(2)}) collective-permute-start(bf16[512,1152]{1,0:T(8,128)(2,1)S(1)} %collective-permute-done.other_ref), channel_id=1, source_target_pairs={{0,1},{1,0},{2,3},{3,2},{4,5},{5,4},{6,7},{7,6},{8,9},{9,8},{10,11... | collective-permute-start | bytes 3538952 | tf_op jit(solution)/shard_map/ppermute | solution.py:242
  39.1 11.0 %collective-permute-done.4.other_ref = bf16[512,1152]{1,0:T(8,128)(2,1)S(1)} collective-permute-done((bf16[512,1152]{1,0:T(8,128)(2,1)S(1)}, bf16[512,1152]{1,0:T(8,128)(2,1)S(1)}, u32[]{:S(2)}, u32[]{:S(2)}) %collective-permute-start.4) | collective-permute-done | bytes 1179680 | tf_op jit(solution)/shard_map/ppermute | solution.py:240
  50.1 8.2 %collective-permute-start.6 = (bf16[512,1152]{1,0:T(8,128)(2,1)S(1)}, bf16[512,1152]{1,0:T(8,128)(2,1)S(1)}, u32[]{:S(2)}, u32[]{:S(2)}) collective-permute-start(bf16[512,1152]{1,0:T(8,128)(2,1)S(1)} %collective-permute-done.4.other_ref), channel_id=1, source_target_pairs={{0,1},{1,0},{2,3},{3,2},{4,5},{5,4},{6,7},{7,6},{8,9},{9,8},{10,11... | collective-permute-start | bytes 3538952 | tf_op jit(solution)/shard_map/ppermute | solution.py:246
  58.3 2.3 %collective-permute-start.1 = (bf16[512,1152]{1,0:T(8,128)(2,1)S(1)}, bf16[512,1152]{1,0:T(8,128)(2,1)S(1)}, u32[]{:S(2)}, u32[]{:S(2)}) collective-permute-start(bf16[512,1152]{1,0:T(8,128)(2,1)S(1)} %collective-permute-done.other_ref), channel_id=1, source_target_pairs={{0,2},{1,511},{2,4},{3,1},{4,6},{5,3},{6,8},{7,5},{8,10},{9,7},{10... | collective-permute-start | bytes 3538952 | tf_op jit(solution)/shard_map/ppermute | solution.py:241
  60.6 3.0 %shard_map.80 = (f32[512,1152]{1,0:T(8,128)S(1)}, f32[512,128]{1,0:T(8,128)S(1)}) custom-call(bf16[512,1152]{1,0:T(8,128)(2,1)S(1)} %shard_map.76.own_ref, bf16[512,1152]{1,0:T(8,128)(2,1)S(1)} %collective-permute-done.other_ref, f32[1]{0:T(128)S(6)} %copy.30.log_scale_ref, f32[1]{0:T(128)S(6)} %copy.31.bias_ref, ...), custom_call_target="tpu_custom_call", output_to_operand_aliasing={{0}: (4, {}), {1}: (5, {})} | custom-call | flops 1207959552 | tf_op jit(solution)/shard_map/pallas_call | solution.py:227
  63.6 0.0 collective-permute-done.5.other_ref
  63.6 3.0 %shard_map.81 = (f32[512,1152]{1,0:T(8,128)S(1)}, f32[512,128]{1,0:T(8,128)S(1)}) custom-call(bf16[512,1152]{1,0:T(8,128)(2,1)S(1)} %shard_map.77.own_ref, bf16[512,1152]{1,0:T(8,128)(2,1)S(1)} %collective-permute-done.5.other_ref, f32[1]{0:T(128)S(6)} %copy.30.log_scale_ref, f32[1]{0:T(128)S(6)} %copy.31.bias_ref, ...), custom_call_target="tpu_custom_call", output_to_operand_aliasing={{0}: (4, {}), {1}: (5, {})} | custom-call | flops 1207959552 | tf_op jit(solution)/shard_map/pallas_call | solution.py:227
  66.6 3.0 %shard_map.82 = (f32[512,1152]{1,0:T(8,128)S(1)}, f32[512,128]{1,0:T(8,128)S(1)}) custom-call(bf16[512,1152]{1,0:T(8,128)(2,1)S(1)} %shard_map.76.own_ref, bf16[512,1152]{1,0:T(8,128)(2,1)S(1)} %collective-permute-done.4.other_ref, f32[1]{0:T(128)S(6)} %copy.30.log_scale_ref, f32[1]{0:T(128)S(6)} %copy.31.bias_ref, ...), custom_call_target="tpu_custom_call", output_to_operand_aliasing={{0}: (4, {}), {1}: (5, {})} | custom-call | flops 1207959552 | tf_op jit(solution)/shard_map/pallas_call | solution.py:227
  69.6 0.0 collective-permute-done.6.other_ref
  69.6 3.9 %shard_map.83 = (f32[512,128]{1,0:T(8,128)S(1)}, bf16[512,1152]{1,0:T(8,128)(2,1)}, bf16[512,1152]{1,0:T(8,128)(2,1)}) custom-call(bf16[512,1152]{1,0:T(8,128)(2,1)S(1)} %shard_map.77.own_ref, bf16[512,1152]{1,0:T(8,128)(2,1)S(1)} %collective-permute-done.6.other_ref, f32[1]{0:T(128)S(6)} %copy.30.log_scale_ref, ...), custom_call_target="tpu_custom_call", output_to_operand_aliasing={{0}: (5, {})} | custom-call | flops 1207959552 | tf_op jit(solution)/shard_map/pallas_call | solution.py:248
  73.5 2.1 %collective-permute-done.1.other_ref = bf16[512,1152]{1,0:T(8,128)(2,1)S(1)} collective-permute-done((bf16[512,1152]{1,0:T(8,128)(2,1)S(1)}, bf16[512,1152]{1,0:T(8,128)(2,1)S(1)}, u32[]{:S(2)}, u32[]{:S(2)}) %collective-permute-start.1) | collective-permute-done | bytes 1179680 | tf_op jit(solution)/shard_map/ppermute | solution.py:241
  75.6 4.3 %shard_map.84 = (f32[1,512]{1,0:T(1,128)}, bf16[512,1152]{1,0:T(8,128)(2,1)}, bf16[512,1152]{1,0:T(8,128)(2,1)}) custom-call(bf16[512,1152]{1,0:T(8,128)(2,1)S(1)} %shard_map.76.own_ref, bf16[512,1152]{1,0:T(8,128)(2,1)S(1)} %collective-permute-done.1.other_ref, f32[1]{0:T(128)S(6)} %copy.30.log_scale_ref, ...), custom_call_target="tpu_custom_call", output_to_operand_aliasing={{1}: (6, {}), {2}: (7, {})} | custom-call | flops 1207959552 | tf_op jit(solution)/shard_map/pallas_call | solution.py:258
Async XLA Ops:
  0.6 1.3 %copy-start = (bf16[512,1152]{1,0:T(8,128)(2,1)S(1)}, bf16[512,1152]{1,0:T(8,128)(2,1)}, u32[]{:S(2)}) copy-start(bf16[512,1152]{1,0:T(8,128)(2,1)} %image_ref.1) | copy-start | bytes 3538948
  1.9 1.3 %copy-start.1 = (bf16[512,1152]{1,0:T(8,128)(2,1)S(1)}, bf16[512,1152]{1,0:T(8,128)(2,1)}, u32[]{:S(2)}) copy-start(bf16[512,1152]{1,0:T(8,128)(2,1)} %text_ref.1) | copy-start | bytes 3538948
  3.4 11.0 %copy-start.2 = (s32[512]{0:T(512)S(1)}, s32[512]{0:T(512)}, u32[]{:S(2)}) copy-start(s32[512]{0:T(512)} %param.7) | copy-start | bytes 6148
  3.7 26.0 %collective-permute-start.2 = (bf16[512,1152]{1,0:T(8,128)(2,1)S(1)}, bf16[512,1152]{1,0:T(8,128)(2,1)S(1)}, u32[]{:S(2)}, u32[]{:S(2)}) collective-permute-start(bf16[512,1152]{1,0:T(8,128)(2,1)S(1)} %shard_map.77.own_ref), channel_id=1, source_target_pairs={{0,1},{1,0},{2,3},{3,2},{4,5},{5,4},{6,7},{7,6},{8,9},{9,8},{10,11... | collective-permute-start | bytes 3538952 | tf_op jit(solution)/shard_map/ppermute | solution.py:209
  12.5 23.4 %collective-permute-start = (bf16[512,1152]{1,0:T(8,128)(2,1)S(1)}, bf16[512,1152]{1,0:T(8,128)(2,1)S(1)}, u32[]{:S(2)}, u32[]{:S(2)}) collective-permute-start(bf16[512,1152]{1,0:T(8,128)(2,1)S(1)} %shard_map.76.own_ref), channel_id=1, source_target_pairs={{0,511},{1,2},{2,1},{3,4},{4,3},{5,6},{6,5},{7,8},{8,7},{9,10},{10... | collective-permute-start | bytes 3538952 | tf_op jit(solution)/shard_map/ppermute | solution.py:207
  14.5 15.3 %collective-permute-start.3 = (s32[512]{0:T(512)S(1)}, s32[512]{0:T(512)S(1)}, u32[]{:S(2)}, u32[]{:S(2)}) collective-permute-start(s32[512]{0:T(512)S(1)} %copy-done.2), channel_id=1, source_target_pairs={{0,1},{1,0},{2,3},{3,2},{4,5},{5,4},{6,7},{7,6},{8,9},{9,8},{10,11... | collective-permute-start | bytes 6152 | tf_op jit(solution)/shard_map/ppermute | solution.py:210
  32.9 17.2 %collective-permute-start.4 = (bf16[512,1152]{1,0:T(8,128)(2,1)S(1)}, bf16[512,1152]{1,0:T(8,128)(2,1)S(1)}, u32[]{:S(2)}, u32[]{:S(2)}) collective-permute-start(bf16[512,1152]{1,0:T(8,128)(2,1)S(1)} %shard_map.77.own_ref), channel_id=1, source_target_pairs={{0,2},{1,511},{2,4},{3,1},{4,6},{5,3},{6,8},{7,5},{8,10},{9,7},{10... | collective-permute-start | bytes 3538952 | tf_op jit(solution)/shard_map/ppermute | solution.py:240
  35.9 27.7 %collective-permute-start.5 = (bf16[512,1152]{1,0:T(8,128)(2,1)S(1)}, bf16[512,1152]{1,0:T(8,128)(2,1)S(1)}, u32[]{:S(2)}, u32[]{:S(2)}) collective-permute-start(bf16[512,1152]{1,0:T(8,128)(2,1)S(1)} %collective-permute-done.other_ref), channel_id=1, source_target_pairs={{0,1},{1,0},{2,3},{3,2},{4,5},{5,4},{6,7},{7,6},{8,9},{9,8},{10,11... | collective-permute-start | bytes 3538952 | tf_op jit(solution)/shard_map/ppermute | solution.py:242
  50.1 19.4 %collective-permute-start.6 = (bf16[512,1152]{1,0:T(8,128)(2,1)S(1)}, bf16[512,1152]{1,0:T(8,128)(2,1)S(1)}, u32[]{:S(2)}, u32[]{:S(2)}) collective-permute-start(bf16[512,1152]{1,0:T(8,128)(2,1)S(1)} %collective-permute-done.4.other_ref), channel_id=1, source_target_pairs={{0,1},{1,0},{2,3},{3,2},{4,5},{5,4},{6,7},{7,6},{8,9},{9,8},{10,11... | collective-permute-start | bytes 3538952 | tf_op jit(solution)/shard_map/ppermute | solution.py:246
  58.3 17.2 %collective-permute-start.1 = (bf16[512,1152]{1,0:T(8,128)(2,1)S(1)}, bf16[512,1152]{1,0:T(8,128)(2,1)S(1)}, u32[]{:S(2)}, u32[]{:S(2)}) collective-permute-start(bf16[512,1152]{1,0:T(8,128)(2,1)S(1)} %collective-permute-done.other_ref), channel_id=1, source_target_pairs={{0,2},{1,511},{2,4},{3,1},{4,6},{5,3},{6,8},{7,5},{8,10},{9,7},{10... | collective-permute-start | bytes 3538952 | tf_op jit(solution)/shard_map/ppermute | solution.py:241

commit v3 on v2

v3 whole, which is shorter than its diff:
```python
import functools

import jax
import jax.numpy as jnp
from jax import lax
from jax.experimental import pallas as pl
from jax.experimental.pallas import tpu as pltpu
from jax.sharding import PartitionSpec as P

STEPS = 4
DIGITS = 3
AXES = ("rows", "cols")
LANES = 128
SPARE = 16
VMEM_LIMIT = 24 * 1024 * 1024


def swap_in_chip(size):
    return [(i, i ^ 1) for i in range(size)]


def swap_across(size):
    return [(i, (i + 1) % size if i % 2 else (i - 1) % size) for i in range(size)]


def two_along(size):
    return [(i, (i - 2) % size if i % 2 else (i + 2) % size) for i in range(size)]


def after(array, *others):
    return lax.optimization_barrier((array,) + others)[0]


def is_even():
    return lax.rem(lax.axis_index("cols"), 2) == 0


def product(left, right, over_left, over_right):
    return lax.dot_general(
        left, right, (((over_left,), (over_right,)), ((), ())), preferred_element_type=jnp.float32
    )


def scale_of(log_scale_ref):
    return jnp.exp(jnp.full((1, LANES), log_scale_ref[0], jnp.float32))[:, :1]


def fold(terms):
    total = terms[:, :LANES]
    for at in range(LANES, terms.shape[1], LANES):
        total = total + terms[:, at : at + LANES]
    return total


def terms_and_slopes(logits, positive=None):
    small = jnp.exp(-jnp.abs(logits))
    terms = jnp.maximum(logits, 0.0) + jnp.log1p(small)
    slopes = jnp.where(logits >= 0, 1.0, small) / (1.0 + small)
    if positive is not None:
        terms = terms - jnp.where(positive, logits, 0.0)
        slopes = slopes - jnp.where(positive, 1.0, 0.0)
    return terms, slopes.astype(jnp.bfloat16)


def copy_by_parity(if_even, if_odd, out, sem):
    even = is_even()
    copies = [(even, pltpu.make_async_copy(if_even, out, sem)), (jnp.logical_not(even), pltpu.make_async_copy(if_odd, out, sem))]
    for here, copy in copies:
        pl.when(here)(copy.start)

    def wait():
        for here, copy in copies:
            pl.when(here)(copy.wait)

    return wait


def ahead_place_kernel(even_ref, odd_ref, out_ref, sem):
    rows, width = even_ref.shape
    wait = copy_by_parity(even_ref, odd_ref, out_ref.at[:rows, :], sem)
    out_ref[rows:, :] = jnp.zeros((SPARE, width), out_ref.dtype)
    wait()


def beside_place_kernel(even_ref, odd_ref, ids_ref, out_ref, with_ids_ref, sems):
    rows, width = even_ref.shape
    waits = [
        copy_by_parity(even_ref, odd_ref, with_ids_ref.at[:rows, :], sems.at[0]),
        copy_by_parity(even_ref, odd_ref, out_ref, sems.at[1]),
    ]
    spare = jnp.zeros((SPARE, width), jnp.float32)
    at_row = lax.broadcasted_iota(jnp.int32, (SPARE, rows), 0)
    ids = jnp.broadcast_to(ids_ref[...], (SPARE, rows))
    digits = jnp.zeros((SPARE, rows), jnp.int32)
    for digit in range(DIGITS):
        digits = jnp.where(at_row == digit, lax.shift_right_logical(ids, 6 * digit) & 63, digits)
    spare = jnp.concatenate([digits.astype(jnp.float32), spare[:, rows:]], axis=1)
    with_ids_ref[rows:, :] = spare.astype(with_ids_ref.dtype)
    for wait in waits:
        wait()


def read_ids(with_ids_ref, rows):
    spare = with_ids_ref[rows:, :][:, :rows].astype(jnp.float32)
    place = lax.broadcasted_iota(jnp.int32, (SPARE, rows), 0)
    weights = jnp.zeros((SPARE, rows), jnp.float32)
    for digit in range(DIGITS):
        weights = jnp.where(place == digit, float(64**digit), weights)
    return jnp.sum(spare * weights, axis=0, keepdims=True).astype(jnp.int32)


def ids_down(ids):
    return jnp.broadcast_to(ids, (LANES, ids.shape[1])).T


def match(down, ids):
    parts = [down == ids[:, at : at + LANES] for at in range(0, ids.shape[1], LANES)]
    return jnp.concatenate(parts, axis=1)


def halves(rows):
    return [slice(0, rows // 2), slice(rows // 2, rows)]


def block_rows(ref, like):
    return ref.at[: like.shape[0], :]


def own_kernel(ahead_ref, beside_ref, ids_ref, log_scale_ref, bias_ref, ahead_total, beside_total, loss_ref, slopes_ref):
    scale, shift = scale_of(log_scale_ref), bias_ref[0]
    ids = ids_ref[...]
    down = ids_down(ids)
    ahead_ref = block_rows(ahead_ref, beside_ref)

    def parts(image_ref, text_ref, image_total, text_total):
        for chunk in halves(image_ref.shape[0]):
            logits = scale * product(image_ref[chunk, :], text_ref[...], 1, 1) + shift
            terms, slopes = terms_and_slopes(logits, match(down[chunk, :], ids))
            loss_ref[chunk, :] = fold(terms)
            slopes_ref[chunk, :] = slopes
            image_total[chunk, :] = product(slopes, text_ref[...], 1, 0)
        text_total[...] = product(slopes_ref[...], image_ref[...], 0, 0)

    even = is_even()

    @pl.when(even)
    def _():
        parts(ahead_ref, beside_ref, ahead_total, beside_total)

    @pl.when(jnp.logical_not(even))
    def _():
        parts(beside_ref, ahead_ref, beside_total, ahead_total)


def pair(own_ref, other_ref, log_scale_ref, bias_ref, total_in, loss_in, loss_ref, image_if_even, store, ids=None):
    scale, shift = scale_of(log_scale_ref), bias_ref[0]
    own_ref, other_ref = block_rows(own_ref, total_in), block_rows(other_ref, total_in)
    counted = jnp.where(is_even() == image_if_even, 1.0, 0.0)
    down = None if ids is None else ids_down(ids[0])
    chunks = halves(own_ref.shape[0])

    def scores(chunk):
        return scale * product(own_ref[chunk, :], other_ref[...], 1, 1) + shift

    logits = scores(chunks[0])
    for at, chunk in enumerate(chunks):
        positive = None if ids is None else match(down[chunk, :], ids[1])
        terms, slopes = terms_and_slopes(logits, positive)
        loss_ref[chunk, :] = loss_in[chunk, :] + counted * fold(terms)
        if at + 1 < len(chunks):
            logits = scores(chunks[at + 1])
        store(chunk, total_in[chunk, :] + product(slopes, other_ref[...], 1, 0))


def keep(total_ref):
    def store(chunk, total):
        total_ref[chunk, :] = total

    return store


def near_kernel(own_ref, other_ref, ids_ref, log_scale_ref, bias_ref, total_in, loss_in, total_ref, loss_ref):
    pair(own_ref, other_ref, log_scale_ref, bias_ref, total_in, loss_in, loss_ref, False, keep(total_ref), (ids_ref[...], read_ids(other_ref, total_in.shape[0])))


def far_kernel(image_if_even, own_ref, other_ref, log_scale_ref, bias_ref, total_in, loss_in, total_ref, loss_ref):
    pair(own_ref, other_ref, log_scale_ref, bias_ref, total_in, loss_in, loss_ref, image_if_even, keep(total_ref))


class Writer:
    def __init__(self, log_scale_ref, rounded_ref, sems, if_even, if_odd):
        self.scale = scale_of(log_scale_ref)
        self.rounded, self.sems, self.outs = rounded_ref, sems, (if_even, if_odd)
        self.chunks = []

    def copies(self, chunk, at):
        even = is_even()
        for out, here in zip(self.outs, (even, jnp.logical_not(even)), strict=True):
            copy = pltpu.make_async_copy(self.rounded.at[chunk, :], out.at[chunk, :], self.sems.at[at])
            yield here, copy

    def __call__(self, chunk, total):
        self.rounded[chunk, :] = (self.scale * total).astype(jnp.bfloat16)
        for here, copy in self.copies(chunk, len(self.chunks)):
            pl.when(here)(copy.start)
        self.chunks.append(chunk)

    def finish(self):
        for at, chunk in enumerate(self.chunks):
            for here, copy in self.copies(chunk, at):
                pl.when(here)(copy.wait)


def beside_kernel(own_ref, other_ref, log_scale_ref, bias_ref, total_in, loss_in, loss_ref, image_ref, text_ref, rounded_ref, sems):
    writer = Writer(log_scale_ref, rounded_ref, sems, text_ref, image_ref)
    pair(own_ref, other_ref, log_scale_ref, bias_ref, total_in, loss_in, loss_ref, False, writer)
    writer.finish()


def ahead_kernel(own_ref, other_ref, log_scale_ref, bias_ref, total_in, loss_in, image_in, text_in, row_loss_ref, image_ref, text_ref, loss_ref, rounded_ref, sems):
    del image_in, text_in
    writer = Writer(log_scale_ref, rounded_ref, sems, image_ref, text_ref)
    pair(own_ref, other_ref, log_scale_ref, bias_ref, total_in, loss_in, loss_ref, True, writer)
    rows = loss_ref.shape[0]
    row_loss_ref[...] = jnp.sum(loss_ref[...].T, axis=0, keepdims=True) / (STEPS * rows)
    writer.finish()


def call(kernel, out_shape, in_specs, out_specs, scratch=(), aliases=None):
    return pl.pallas_call(
        kernel,
        out_shape=out_shape,
        in_specs=in_specs,
        out_specs=out_specs,
        scratch_shapes=scratch,
        input_output_aliases=aliases or {},
        cost_estimate=pl.CostEstimate(flops=1, bytes_accessed=1, transcendentals=0),
        compiler_params=pltpu.CompilerParams(vmem_limit_bytes=VMEM_LIMIT),
    )


def near(array):
    return pltpu.with_memory_space_constraint(array, pltpu.VMEM)


def local(image, text, ids, log_scale, logit_bias):
    size = lax.axis_size(AXES)
    rows, width = image.shape
    in_vmem = pl.BlockSpec(memory_space=pltpu.VMEM)
    in_smem = pl.BlockSpec(memory_space=pltpu.SMEM)
    anywhere = pl.BlockSpec(memory_space=pl.ANY)
    total_shape = pltpu.VMEM((rows, width), jnp.float32)
    loss_shape = pltpu.VMEM((rows, LANES), jnp.float32)
    grad_shape = jax.ShapeDtypeStruct((rows, width), jnp.bfloat16)
    in_hbm = lambda array: pltpu.with_memory_space_constraint(array, pltpu.HBM)
    sems = pltpu.SemaphoreType.DMA((2,))

    ahead = call(
        ahead_place_kernel,
        pltpu.VMEM((rows + SPARE, width), jnp.bfloat16),
        [anywhere] * 2,
        in_vmem,
        [pltpu.SemaphoreType.DMA],
    )(in_hbm(image), in_hbm(text))
    cross1 = lax.ppermute(ahead, AXES, swap_across(size))

    ids = ids.reshape(1, rows)
    beside, with_ids = call(
        beside_place_kernel,
        (pltpu.VMEM((rows, width), jnp.bfloat16), pltpu.VMEM((rows + SPARE, width), jnp.bfloat16)),
        [anywhere] * 2 + [in_vmem],
        (in_vmem, in_vmem),
        [sems],
    )(in_hbm(text), in_hbm(after(image, ahead)), ids)
    chip1 = lax.ppermute(with_ids, AXES, swap_in_chip(size))

    ahead_total, beside_total, loss = call(
        own_kernel,
        (total_shape, total_shape, loss_shape),
        [in_vmem] * 3 + [in_smem] * 2,
        (in_vmem, in_vmem, in_vmem),
        [pltpu.VMEM((rows, rows), jnp.bfloat16)],
    )(near(ahead), near(beside), ids, log_scale, logit_bias)
    cross2 = lax.ppermute(after(beside, loss), AXES, two_along(size))

    far_specs = [in_vmem] * 2 + [in_smem] * 2 + [in_vmem] * 2

    def far(image_if_even, own, other, total, loss):
        return call(
            functools.partial(far_kernel, image_if_even), (total_shape, loss_shape), far_specs, (in_vmem, in_vmem), aliases={4: 0, 5: 1}
        )(near(own), near(other), log_scale, logit_bias, near(total), near(loss))

    beside_total, loss = call(
        near_kernel,
        (total_shape, loss_shape),
        [in_vmem] * 3 + [in_smem] * 2 + [in_vmem] * 2,
        (in_vmem, in_vmem),
        aliases={5: 0, 6: 1},
    )(near(beside), near(chip1), ids, log_scale, logit_bias, near(beside_total), near(loss))

    cross3 = lax.ppermute(cross1, AXES, two_along(size))
    chip2 = lax.ppermute(cross1[:rows], AXES, swap_in_chip(size))
    ahead_total, loss = far(True, ahead, cross1, ahead_total, loss)
    chip3 = lax.ppermute(after(cross2, loss), AXES, swap_in_chip(size))
    beside_total, loss = far(False, beside, chip2, beside_total, loss)
    ahead_total, loss = far(True, ahead, cross2, ahead_total, loss)
    loss, grad_image, grad_text = call(
        beside_kernel,
        (loss_shape, grad_shape, grad_shape),
        far_specs,
        (in_vmem, anywhere, anywhere),
        [pltpu.VMEM((rows, width), jnp.bfloat16), sems],
        aliases={5: 0},
    )(near(beside), near(chip3), log_scale, logit_bias, near(beside_total), near(loss))

    row_loss, grad_image, grad_text = call(
        ahead_kernel,
        (jax.ShapeDtypeStruct((1, rows), jnp.float32), grad_shape, grad_shape),
        far_specs + [anywhere] * 2,
        (in_vmem, anywhere, anywhere),
        [pltpu.VMEM((rows, LANES), jnp.float32), pltpu.VMEM((rows, width), jnp.bfloat16), sems],
        aliases={6: 1, 7: 2},
    )(near(ahead), near(cross3), log_scale, logit_bias, near(ahead_total), near(loss), grad_image, grad_text)
    return row_loss.reshape(rows), grad_image, grad_text


def solution(mesh):
    in_specs = (P(AXES, None), P(AXES, None), P(AXES), P(), P())
    out_specs = (P(AXES), P(AXES, None), P(AXES, None))
    return jax.shard_map(local, mesh=mesh, in_specs=in_specs, out_specs=out_specs, check_vma=False)
```

time: 81.5 us -> 64.5 us (0.79); the launches traced: 80.1 us -> 64.2 us
  waiting for transfers between devices: 13.1 us -> 0.02 us
  local copies, waits for them, and re-layouts: 2.54 us -> 0.1 us
  Pallas kernels: 24 us -> 21.9 us
  starting transfers between devices: 38.2 us -> 39.9 us
    ppermute x4 -> x3, starting transfers between devices: 31 us -> 19 us  [the longest x1 14.5 us: local(): chip1 = lax.ppermute(with_ids, AXES, swap_in_chip(size))]
    ppermute x1, starting transfers between devices: 2.27 us -> 13.3 us  [local(): cross3 = lax.ppermute(cross1, AXES, two_along(size))]
    ppermute x1, waiting for transfers between devices: 11 us -> 0.01 us  [local(): cross2 = lax.ppermute(after(beside, loss), AXES, two_along(size))]
    ppermute x1, starting transfers between devices: 1.92 us -> 4.59 us  [local(): cross1 = lax.ppermute(ahead, AXES, swap_across(size))]
    unnamed x6 -> x2, local copies, waits for them, and re-layouts: 2.54 us -> 0.01 us
    pallas_call x3, Pallas kernels: 8.92 us -> 6.72 us  [far(): call(functools.partial(far_kernel, image_if_even), (total_shape, loss_sha...]
    ppermute x1, waiting for transfers between devices: 2.11 us -> 0.01 us  [local(): cross3 = lax.ppermute(cross1, AXES, two_along(size))]
    pallas_call x3, Pallas kernels: 3.64 us -> 5.43 us  [the longest x1 2.46 us: local(): call(near_kernel, (total_shape, loss_shape), [in_vmem] * 3 + [in_smem] *...]
  transfers between devices with their start and end apart: 7 -> 6, of which waited for: 2 -> 0; matrix products, arithmetic and copies ran while one was open for 0% -> 0% of each run, Pallas kernels for 24% -> 27%
where the time goes in v3:
time: 64.5 us; the launch traced here: 64.2 us
  starting transfers between devices  39.9 us (62%)
  Pallas kernels  21.9 us (34%)
  between operations  2.26 us (4%)
    ppermute x1, starting transfers between devices, local(): chip1 = lax.ppermute(with_ids, AXES, swap_in_chip(size))  14.5 us
    ppermute x1, starting transfers between devices, local(): cross3 = lax.ppermute(cross1, AXES, two_along(size))  13.3 us
    pallas_call x3, Pallas kernels, far(): call(functools.partial(far_kernel, image_if_even), (total_shape, loss_sha...  6.72 us
    ppermute x1, starting transfers between devices, local(): cross1 = lax.ppermute(ahead, AXES, swap_across(size))  4.59 us
    pallas_call x1, Pallas kernels, local(): call(ahead_kernel, (jax.ShapeDtypeStruct((1, rows), jnp.float32), grad_sh...  3.54 us
    pallas_call x1, Pallas kernels, local(): call(own_kernel, (total_shape, total_shape, loss_shape), [in_vmem] * 3 +...  3.28 us
    ppermute x1, starting transfers between devices, local(): cross2 = lax.ppermute(after(beside, loss), AXES, two_along(size))  2.99 us
    pallas_call x1, Pallas kernels, local(): call(beside_kernel, (loss_shape, grad_shape, grad_shape), far_specs, (in_...  2.93 us
  transfers between devices with their start and end apart: 6, of which 0 were waited for; matrix products, arithmetic and copies ran while one was open for 0% of the time, Pallas kernels for 27%

profile of v3, /device:TPU:1, one launch (start us, length us, event | category | flops | bytes accessed | tf_op | source)
XLA Modules:
  0.0 64.2 jit_solution(10274959470038326021)
XLA Ops:
  0.6 0.0 copy-start
  0.6 1.3 %shard_map.76.ahead_ref.own_ref = bf16[528,1152]{1,0:T(8,128)(2,1)S(1)} custom-call(bf16[512,1152]{1,0:T(8,128)(2,1)} %odd_ref.2, bf16[512,1152]{1,0:T(8,128)(2,1)} %even_ref.3), custom_call_target="tpu_custom_call" | custom-call | flops 1 | bytes 1 | tf_op jit(solution)/shard_map/pallas_call | solution.py:258
  1.9 4.6 %collective-permute-start = (bf16[528,1152]{1,0:T(8,128)(2,1)S(1)}, bf16[528,1152]{1,0:T(8,128)(2,1)S(1)}, u32[]{:S(2)}, u32[]{:S(2)}) collective-permute-start(bf16[528,1152]{1,0:T(8,128)(2,1)S(1)} %shard_map.76.ahead_ref.own_ref), channel_id=1, source_target_pairs={{0,511},{1,2},{2,1},{3,4},{4,3},{5,6},{6,5},{7,8},{8,7},{9,10},{10... | collective-permute-start | bytes 3649544 | tf_op jit(solution)/shard_map/ppermute | solution.py:265
  6.5 0.0 copy-done
  6.5 1.7 %shard_map.77 = (bf16[512,1152]{1,0:T(8,128)(2,1)S(1)}, bf16[528,1152]{1,0:T(8,128)(2,1)S(1)}) custom-call(bf16[512,1152]{1,0:T(8,128)(2,1)} %even_ref.3, bf16[512,1152]{1,0:T(8,128)(2,1)} %odd_ref.2, s32[1,512]{1,0:T(1,128)S(1)} %bitcast.2), custom_call_target="tpu_custom_call" | custom-call | flops 1 | bytes 1 | tf_op jit(solution)/shard_map/pallas_call | solution.py:268
  8.2 14.5 %collective-permute-start.3 = (bf16[528,1152]{1,0:T(8,128)(2,1)S(1)}, bf16[528,1152]{1,0:T(8,128)(2,1)S(1)}, u32[]{:S(2)}, u32[]{:S(2)}) collective-permute-start(bf16[528,1152]{1,0:T(8,128)(2,1)S(1)} %get-tuple-element.30), channel_id=1, source_target_pairs={{0,1},{1,0},{2,3},{3,2},{4,5},{5,4},{6,7},{7,6},{8,9},{9,8},{10,11... | collective-permute-start | bytes 3649544 | tf_op jit(solution)/shard_map/ppermute | solution.py:275
  24.0 3.3 %shard_map.78 = (f32[512,1152]{1,0:T(8,128)S(1)}, f32[512,1152]{1,0:T(8,128)S(1)}, f32[512,128]{1,0:T(8,128)S(1)}) custom-call(bf16[528,1152]{1,0:T(8,128)(2,1)S(1)} %shard_map.76.ahead_ref.own_ref, bf16[512,1152]{1,0:T(8,128)(2,1)S(1)} %get-tuple-element.28.beside_ref.own_ref, s32[1,512]{1,0:T(1,128)S(1)} %bitcast.3, f32[1]{0:T(128)S(6)} %copy.30.log_scale_ref, ...), custom_call_target="tpu_custom_call" | custom-call | flops 1 | bytes 1 | tf_op jit(solution)/shard_map/pallas_call | solution.py:277
  27.3 3.0 %collective-permute-start.2 = (bf16[512,1152]{1,0:T(8,128)(2,1)S(1)}, bf16[512,1152]{1,0:T(8,128)(2,1)S(1)}, u32[]{:S(2)}, u32[]{:S(2)}) collective-permute-start(bf16[512,1152]{1,0:T(8,128)(2,1)S(1)} %get-tuple-element.28.beside_ref.own_ref), channel_id=1, source_target_pairs={{0,2},{1,511},{2,4},{3,1},{4,6},{5,3},{6,8},{7,5},{8,10},{9,7},{10... | collective-permute-start | bytes 3538952 | tf_op jit(solution)/shard_map/ppermute | solution.py:284
  30.3 0.0 collective-permute-done.other_ref
  30.3 13.3 %collective-permute-start.1 = (bf16[528,1152]{1,0:T(8,128)(2,1)S(1)}, bf16[528,1152]{1,0:T(8,128)(2,1)S(1)}, u32[]{:S(2)}, u32[]{:S(2)}) collective-permute-start(bf16[528,1152]{1,0:T(8,128)(2,1)S(1)} %collective-permute-done.other_ref), channel_id=1, source_target_pairs={{0,2},{1,511},{2,4},{3,1},{4,6},{5,3},{6,8},{7,5},{8,10},{9,7},{10... | collective-permute-start | bytes 3649544 | tf_op jit(solution)/shard_map/ppermute | solution.py:301
  43.7 0.1 slice.4
  43.8 1.9 %collective-permute-start.4 = (bf16[512,1152]{1,0:T(8,128)(2,1)S(1)}, bf16[512,1152]{1,0:T(8,128)(2,1)S(1)}, u32[]{:S(2)}, u32[]{:S(2)}) collective-permute-start(bf16[512,1152]{1,0:T(8,128)(2,1)S(1)} %slice.4), channel_id=1, source_target_pairs={{0,1},{1,0},{2,3},{3,2},{4,5},{5,4},{6,7},{7,6},{8,9},{9,8},{10,11... | collective-permute-start | bytes 3538952 | tf_op jit(solution)/shard_map/ppermute | solution.py:302
  45.7 0.0 collective-permute-done.3.other_ref
  45.7 2.5 %shard_map.79 = (f32[512,1152]{1,0:T(8,128)S(1)}, f32[512,128]{1,0:T(8,128)S(1)}) custom-call(bf16[512,1152]{1,0:T(8,128)(2,1)S(1)} %get-tuple-element.28.beside_ref.own_ref, bf16[528,1152]{1,0:T(8,128)(2,1)S(1)} %collective-permute-done.3.other_ref, s32[1,512]{1,0:T(1,128)S(1)} %bitcast.4, ...), custom_call_target="tpu_custom_call", output_to_operand_aliasing={{0}: (5, {}), {1}: (6, {})} | custom-call | flops 1 | bytes 1 | tf_op jit(solution)/shard_map/pallas_call | solution.py:293
  48.2 2.2 %shard_map.80 = (f32[512,1152]{1,0:T(8,128)S(1)}, f32[512,128]{1,0:T(8,128)S(1)}) custom-call(bf16[528,1152]{1,0:T(8,128)(2,1)S(1)} %shard_map.76.ahead_ref.own_ref, bf16[528,1152]{1,0:T(8,128)(2,1)S(1)} %collective-permute-done.other_ref, f32[1]{0:T(128)S(6)} %copy.30.log_scale_ref, ...), custom_call_target="tpu_custom_call", output_to_operand_aliasing={{0}: (4, {}), {1}: (5, {})} | custom-call | flops 1 | bytes 1 | tf_op jit(solution)/shard_map/pallas_call | solution.py:289
  50.4 0.0 collective-permute-done.2.other_ref
  50.4 2.6 %collective-permute-start.5 = (bf16[512,1152]{1,0:T(8,128)(2,1)S(1)}, bf16[512,1152]{1,0:T(8,128)(2,1)S(1)}, u32[]{:S(2)}, u32[]{:S(2)}) collective-permute-start(bf16[512,1152]{1,0:T(8,128)(2,1)S(1)} %collective-permute-done.2.other_ref), channel_id=1, source_target_pairs={{0,1},{1,0},{2,3},{3,2},{4,5},{5,4},{6,7},{7,6},{8,9},{9,8},{10,11... | collective-permute-start | bytes 3538952 | tf_op jit(solution)/shard_map/ppermute | solution.py:304
  53.0 0.0 collective-permute-done.4.other_ref
  53.0 2.2 %shard_map.81 = (f32[512,1152]{1,0:T(8,128)S(1)}, f32[512,128]{1,0:T(8,128)S(1)}) custom-call(bf16[512,1152]{1,0:T(8,128)(2,1)S(1)} %get-tuple-element.28.beside_ref.own_ref, bf16[512,1152]{1,0:T(8,128)(2,1)S(1)} %collective-permute-done.4.other_ref, f32[1]{0:T(128)S(6)} %copy.30.log_scale_ref, ...), custom_call_target="tpu_custom_call", output_to_operand_aliasing={{0}: (4, {}), {1}: (5, {})} | custom-call | flops 1 | bytes 1 | tf_op jit(solution)/shard_map/pallas_call | solution.py:289
  55.3 2.2 %shard_map.82 = (f32[512,1152]{1,0:T(8,128)S(1)}, f32[512,128]{1,0:T(8,128)S(1)}) custom-call(bf16[528,1152]{1,0:T(8,128)(2,1)S(1)} %shard_map.76.ahead_ref.own_ref, bf16[512,1152]{1,0:T(8,128)(2,1)S(1)} %collective-permute-done.2.other_ref, f32[1]{0:T(128)S(6)} %copy.30.log_scale_ref, ...), custom_call_target="tpu_custom_call", output_to_operand_aliasing={{0}: (4, {}), {1}: (5, {})} | custom-call | flops 1 | bytes 1 | tf_op jit(solution)/shard_map/pallas_call | solution.py:289
  57.5 0.0 collective-permute-done.5.other_ref
  57.5 2.9 %shard_map.83 = (f32[512,128]{1,0:T(8,128)S(1)}, bf16[512,1152]{1,0:T(8,128)(2,1)}, bf16[512,1152]{1,0:T(8,128)(2,1)}) custom-call(bf16[512,1152]{1,0:T(8,128)(2,1)S(1)} %get-tuple-element.28.beside_ref.own_ref, bf16[512,1152]{1,0:T(8,128)(2,1)S(1)} %collective-permute-done.5.other_ref, f32[1]{0:T(128)S(6)} %copy.30.log_scale_ref, ...), custom_call_target="tpu_custom_call", output_to_operand_aliasing={{0}: (5, {})} | custom-call | flops 1 | bytes 1 | tf_op jit(solution)/shard_map/pallas_call | solution.py:307
  60.5 0.0 collective-permute-done.1.other_ref
  60.5 3.5 %shard_map.84 = (f32[1,512]{1,0:T(1,128)}, bf16[512,1152]{1,0:T(8,128)(2,1)}, bf16[512,1152]{1,0:T(8,128)(2,1)}) custom-call(bf16[528,1152]{1,0:T(8,128)(2,1)S(1)} %shard_map.76.ahead_ref.own_ref, bf16[528,1152]{1,0:T(8,128)(2,1)S(1)} %collective-permute-done.1.other_ref, f32[1]{0:T(128)S(6)} %copy.30.log_scale_ref, ...), custom_call_target="tpu_custom_call", output_to_operand_aliasing={{1}: (6, {}), {2}: (7, {})} | custom-call | flops 1 | bytes 1 | tf_op jit(solution)/shard_map/pallas_call | solution.py:316
Async XLA Ops:
  0.6 5.9 %copy-start = (s32[512]{0:T(512)S(1)}, s32[512]{0:T(512)}, u32[]{:S(2)}) copy-start(s32[512]{0:T(512)} %param.7) | copy-start | bytes 6148
  1.9 28.4 %collective-permute-start = (bf16[528,1152]{1,0:T(8,128)(2,1)S(1)}, bf16[528,1152]{1,0:T(8,128)(2,1)S(1)}, u32[]{:S(2)}, u32[]{:S(2)}) collective-permute-start(bf16[528,1152]{1,0:T(8,128)(2,1)S(1)} %shard_map.76.ahead_ref.own_ref), channel_id=1, source_target_pairs={{0,511},{1,2},{2,1},{3,4},{4,3},{5,6},{6,5},{7,8},{8,7},{9,10},{10... | collective-permute-start | bytes 3649544 | tf_op jit(solution)/shard_map/ppermute | solution.py:265
  8.2 37.4 %collective-permute-start.3 = (bf16[528,1152]{1,0:T(8,128)(2,1)S(1)}, bf16[528,1152]{1,0:T(8,128)(2,1)S(1)}, u32[]{:S(2)}, u32[]{:S(2)}) collective-permute-start(bf16[528,1152]{1,0:T(8,128)(2,1)S(1)} %get-tuple-element.30), channel_id=1, source_target_pairs={{0,1},{1,0},{2,3},{3,2},{4,5},{5,4},{6,7},{7,6},{8,9},{9,8},{10,11... | collective-permute-start | bytes 3649544 | tf_op jit(solution)/shard_map/ppermute | solution.py:275
  27.3 23.1 %collective-permute-start.2 = (bf16[512,1152]{1,0:T(8,128)(2,1)S(1)}, bf16[512,1152]{1,0:T(8,128)(2,1)S(1)}, u32[]{:S(2)}, u32[]{:S(2)}) collective-permute-start(bf16[512,1152]{1,0:T(8,128)(2,1)S(1)} %get-tuple-element.28.beside_ref.own_ref), channel_id=1, source_target_pairs={{0,2},{1,511},{2,4},{3,1},{4,6},{5,3},{6,8},{7,5},{8,10},{9,7},{10... | collective-permute-start | bytes 3538952 | tf_op jit(solution)/shard_map/ppermute | solution.py:284
  30.3 30.2 %collective-permute-start.1 = (bf16[528,1152]{1,0:T(8,128)(2,1)S(1)}, bf16[528,1152]{1,0:T(8,128)(2,1)S(1)}, u32[]{:S(2)}, u32[]{:S(2)}) collective-permute-start(bf16[528,1152]{1,0:T(8,128)(2,1)S(1)} %collective-permute-done.other_ref), channel_id=1, source_target_pairs={{0,2},{1,511},{2,4},{3,1},{4,6},{5,3},{6,8},{7,5},{8,10},{9,7},{10... | collective-permute-start | bytes 3649544 | tf_op jit(solution)/shard_map/ppermute | solution.py:301
  43.8 9.3 %collective-permute-start.4 = (bf16[512,1152]{1,0:T(8,128)(2,1)S(1)}, bf16[512,1152]{1,0:T(8,128)(2,1)S(1)}, u32[]{:S(2)}, u32[]{:S(2)}) collective-permute-start(bf16[512,1152]{1,0:T(8,128)(2,1)S(1)} %slice.4), channel_id=1, source_target_pairs={{0,1},{1,0},{2,3},{3,2},{4,5},{5,4},{6,7},{7,6},{8,9},{9,8},{10,11... | collective-permute-start | bytes 3538952 | tf_op jit(solution)/shard_map/ppermute | solution.py:302
  50.4 7.1 %collective-permute-start.5 = (bf16[512,1152]{1,0:T(8,128)(2,1)S(1)}, bf16[512,1152]{1,0:T(8,128)(2,1)S(1)}, u32[]{:S(2)}, u32[]{:S(2)}) collective-permute-start(bf16[512,1152]{1,0:T(8,128)(2,1)S(1)} %collective-permute-done.2.other_ref), channel_id=1, source_target_pairs={{0,1},{1,0},{2,3},{3,2},{4,5},{5,4},{6,7},{7,6},{8,9},{9,8},{10,11... | collective-permute-start | bytes 3538952 | tf_op jit(solution)/shard_map/ppermute | solution.py:304

commit v4 on v3

v4 whole, which is shorter than its diff:
```python
import functools

import jax
import jax.numpy as jnp
from jax import lax
from jax.experimental import pallas as pl
from jax.experimental.pallas import tpu as pltpu
from jax.sharding import PartitionSpec as P

STEPS = 4
DIGITS = 3
AXES = ("rows", "cols")
LANES = 128
SPARE = 16
VMEM_LIMIT = 24 * 1024 * 1024


def swap_in_chip(size):
    return [(i, i ^ 1) for i in range(size)]


def swap_across(size):
    return [(i, (i + 1) % size if i % 2 else (i - 1) % size) for i in range(size)]


def two_along(size):
    return [(i, (i - 2) % size if i % 2 else (i + 2) % size) for i in range(size)]


def after(array, *others):
    return lax.optimization_barrier((array,) + others)[0]


def is_even():
    return lax.rem(lax.axis_index("cols"), 2) == 0


def product(left, right, over_left, over_right):
    return lax.dot_general(
        left, right, (((over_left,), (over_right,)), ((), ())), preferred_element_type=jnp.float32
    )


def scale_and_shift(scalars_ref):
    return scalars_ref[0:1, 0:1], scalars_ref[1:2, 0:1]


def fold(terms):
    total = terms[:, :LANES]
    for at in range(LANES, terms.shape[1], LANES):
        total = total + terms[:, at : at + LANES]
    return total


def by_parity(true_if_even, body):
    even = is_even()

    @pl.when(even)
    def _():
        body(true_if_even)

    @pl.when(jnp.logical_not(even))
    def _():
        body(not true_if_even)


def slopes_of(logits, small, positive=None):
    slopes = jnp.where(logits >= 0, 1.0, small) / (1.0 + small)
    if positive is not None:
        slopes = slopes - jnp.where(positive, 1.0, 0.0)
    return slopes.astype(jnp.bfloat16)


def terms_of(logits, small, positive=None):
    terms = jnp.maximum(logits, 0.0) + jnp.log1p(small)
    if positive is not None:
        terms = terms - jnp.where(positive, logits, 0.0)
    return terms


def copy_by_parity(if_even, if_odd, out, sem):
    even = is_even()
    copies = [(even, pltpu.make_async_copy(if_even, out, sem)), (jnp.logical_not(even), pltpu.make_async_copy(if_odd, out, sem))]
    for here, copy in copies:
        pl.when(here)(copy.start)

    def wait():
        for here, copy in copies:
            pl.when(here)(copy.wait)

    return wait


def ahead_place_kernel(even_ref, odd_ref, out_ref, sem):
    rows, width = even_ref.shape
    wait = copy_by_parity(even_ref, odd_ref, out_ref.at[:rows, :], sem)
    out_ref[rows:, :] = jnp.zeros((SPARE, width), out_ref.dtype)
    wait()


def beside_place_kernel(even_ref, odd_ref, ids_ref, out_ref, sem):
    rows, width = even_ref.shape
    wait = copy_by_parity(even_ref, odd_ref, out_ref.at[:rows, :], sem)
    spare = jnp.zeros((SPARE, width), jnp.float32)
    at_row = lax.broadcasted_iota(jnp.int32, (SPARE, rows), 0)
    ids = jnp.broadcast_to(ids_ref[...], (SPARE, rows))
    digits = jnp.zeros((SPARE, rows), jnp.int32)
    for digit in range(DIGITS):
        digits = jnp.where(at_row == digit, lax.shift_right_logical(ids, 6 * digit) & 63, digits)
    spare = jnp.concatenate([digits.astype(jnp.float32), spare[:, rows:]], axis=1)
    out_ref[rows:, :] = spare.astype(out_ref.dtype)
    wait()


def read_ids(with_ids_ref, rows):
    spare = with_ids_ref[rows:, :][:, :rows].astype(jnp.float32)
    place = lax.broadcasted_iota(jnp.int32, (SPARE, rows), 0)
    weights = jnp.zeros((SPARE, rows), jnp.float32)
    for digit in range(DIGITS):
        weights = jnp.where(place == digit, float(64**digit), weights)
    return jnp.sum(spare * weights, axis=0, keepdims=True).astype(jnp.int32)


def ids_down(ids):
    return jnp.broadcast_to(ids, (LANES, ids.shape[1])).T


def match(down, ids):
    parts = [down == ids[:, at : at + LANES] for at in range(0, ids.shape[1], LANES)]
    return jnp.concatenate(parts, axis=1)


def halves(rows):
    return [slice(0, rows // 2), slice(rows // 2, rows)]


def block_rows(ref, like):
    return ref.at[: like.shape[0], :]


def own_kernel(ahead_ref, with_ids_ref, ids_ref, scalars_ref, beside_ref, slopes_ref, loss_ref, sem):
    beside_copy = pltpu.make_async_copy(block_rows(with_ids_ref, beside_ref), beside_ref, sem)
    beside_copy.start()
    scale, shift = scale_and_shift(scalars_ref)
    ids = ids_ref[...]
    down = ids_down(ids)
    ahead_ref, with_ids_ref = block_rows(ahead_ref, beside_ref), block_rows(with_ids_ref, beside_ref)

    def body(even):
        image_ref, text_ref = (ahead_ref, with_ids_ref) if even else (with_ids_ref, ahead_ref)
        for chunk in halves(image_ref.shape[0]):
            logits = scale * product(image_ref[chunk, :], text_ref[...], 1, 1) + shift
            small, positive = jnp.exp(-jnp.abs(logits)), match(down[chunk, :], ids)
            slopes_ref[chunk, :] = slopes_of(logits, small, positive)
            loss_ref[chunk, :] = fold(terms_of(logits, small, positive))

    by_parity(True, body)
    beside_copy.wait()


def pair(own_ref, other_ref, scalars_ref, total_in, loss_in, loss_ref, image_if_even, store, ids=None):
    scale, shift = scale_and_shift(scalars_ref)
    own_ref, other_ref = block_rows(own_ref, total_in), block_rows(other_ref, total_in)
    down = None if ids is None else ids_down(ids[0])
    chunks = halves(own_ref.shape[0])

    def scores(chunk):
        return scale * product(own_ref[chunk, :], other_ref[...], 1, 1) + shift

    def body(counted):
        logits = scores(chunks[0])
        for at, chunk in enumerate(chunks):
            positive = None if ids is None else match(down[chunk, :], ids[1])
            small = jnp.exp(-jnp.abs(logits))
            slopes = slopes_of(logits, small, positive)
            if counted:
                loss_ref[chunk, :] = loss_in[chunk, :] + fold(terms_of(logits, small, positive))
            else:
                loss_ref[chunk, :] = loss_in[chunk, :]
            if at + 1 < len(chunks):
                logits = scores(chunks[at + 1])
            store(chunk, total_in[chunk, :] + product(slopes, other_ref[...], 1, 0))

    by_parity(image_if_even, body)


def keep(total_ref):
    def store(chunk, total):
        total_ref[chunk, :] = total

    return store


def near_kernel(ahead_ref, own_ref, other_ref, own_slopes_ref, ids_ref, scalars_ref, loss_in, ahead_total, total_ref, loss_ref):
    ahead_ref = block_rows(ahead_ref, own_ref)

    def body(even):
        image_ref, text_ref = (ahead_ref, own_ref) if even else (own_ref, ahead_ref)
        image_total, text_total = (ahead_total, total_ref) if even else (total_ref, ahead_total)
        image_total[...] = product(own_slopes_ref[...], text_ref[...], 1, 0)
        text_total[...] = product(own_slopes_ref[...], image_ref[...], 0, 0)

    by_parity(True, body)
    ids = (ids_ref[...], read_ids(other_ref, own_ref.shape[0]))
    pair(own_ref, other_ref, scalars_ref, total_ref, loss_in, loss_ref, False, keep(total_ref), ids)


def far_kernel(image_if_even, own_ref, other_ref, scalars_ref, total_in, loss_in, total_ref, loss_ref):
    pair(own_ref, other_ref, scalars_ref, total_in, loss_in, loss_ref, image_if_even, keep(total_ref))


def beside_kernel(own_ref, other_ref, scalars_ref, total_in, loss_in, rounded_ref, loss_ref):
    scale, _ = scale_and_shift(scalars_ref)

    def store(chunk, total):
        rounded_ref[chunk, :] = (scale * total).astype(jnp.bfloat16)

    pair(own_ref, other_ref, scalars_ref, total_in, loss_in, loss_ref, False, store)


def ahead_kernel(own_ref, other_ref, scalars_ref, total_in, loss_in, beside_ref, row_loss_ref, image_ref, text_ref, rounded_ref, sems):
    scale, shift = scale_and_shift(scalars_ref)
    own_ref, other_ref = block_rows(own_ref, total_in), block_rows(other_ref, total_in)
    rows = total_in.shape[0]
    chunks = halves(rows)

    def scores(chunk):
        return scale * product(own_ref[chunk, :], other_ref[...], 1, 1) + shift

    def body(even):
        ahead_out, beside_out = (image_ref, text_ref) if even else (text_ref, image_ref)
        copies = [pltpu.make_async_copy(beside_ref, beside_out, sems.at[0])]
        copies[0].start()
        logits = [scores(chunks[0])]
        small = []
        for at, chunk in enumerate(chunks):
            small.append(jnp.exp(-jnp.abs(logits[at])))
            slopes = slopes_of(logits[at], small[at])
            if at + 1 < len(chunks):
                logits.append(scores(chunks[at + 1]))
            total = total_in[chunk, :] + product(slopes, other_ref[...], 1, 0)
            rounded_ref[chunk, :] = (scale * total).astype(jnp.bfloat16)
            copies.append(pltpu.make_async_copy(rounded_ref.at[chunk, :], ahead_out.at[chunk, :], sems.at[at + 1]))
            copies[-1].start()
        for at, chunk in enumerate(chunks):
            loss = loss_in[chunk, :]
            if even:
                loss = loss + fold(terms_of(logits[at], small[at]))
            row_loss_ref[:, chunk] = jnp.sum(loss.T, axis=0, keepdims=True) / (STEPS * rows)
        for copy in copies:
            copy.wait()

    by_parity(True, body)


def call(kernel, out_shape, in_specs, out_specs, scratch=(), aliases=None):
    return pl.pallas_call(
        kernel,
        out_shape=out_shape,
        in_specs=in_specs,
        out_specs=out_specs,
        scratch_shapes=scratch,
        input_output_aliases=aliases or {},
        cost_estimate=pl.CostEstimate(flops=1, bytes_accessed=1, transcendentals=0),
        compiler_params=pltpu.CompilerParams(vmem_limit_bytes=VMEM_LIMIT),
    )


def near(array):
    return pltpu.with_memory_space_constraint(array, pltpu.VMEM)


def local(image, text, ids, log_scale, logit_bias):
    size = lax.axis_size(AXES)
    rows, width = image.shape
    in_vmem = pl.BlockSpec(memory_space=pltpu.VMEM)
    anywhere = pl.BlockSpec(memory_space=pl.ANY)
    total_shape = pltpu.VMEM((rows, width), jnp.float32)
    loss_shape = pltpu.VMEM((rows, LANES), jnp.float32)
    block_shape = pltpu.VMEM((rows, width), jnp.bfloat16)
    grad_shape = jax.ShapeDtypeStruct((rows, width), jnp.bfloat16)
    in_hbm = lambda array: pltpu.with_memory_space_constraint(array, pltpu.HBM)

    ahead = call(
        ahead_place_kernel,
        pltpu.VMEM((rows + SPARE, width), jnp.bfloat16),
        [anywhere] * 2,
        in_vmem,
        [pltpu.SemaphoreType.DMA],
    )(in_hbm(image), in_hbm(text))
    cross1 = lax.ppermute(ahead, AXES, swap_across(size))

    ids = ids.reshape(1, rows)
    with_ids = call(
        beside_place_kernel,
        pltpu.VMEM((rows + SPARE, width), jnp.bfloat16),
        [anywhere] * 2 + [in_vmem],
        in_vmem,
        [pltpu.SemaphoreType.DMA],
    )(in_hbm(text), in_hbm(after(image, ahead)), ids)
    scalars = jnp.where(lax.broadcasted_iota(jnp.int32, (8, LANES), 0) == 0, jnp.exp(log_scale), logit_bias)
    chip1 = lax.ppermute(with_ids, AXES, swap_in_chip(size))

    beside, own_slopes, loss = call(
        own_kernel,
        (block_shape, pltpu.VMEM((rows, rows), jnp.bfloat16), loss_shape),
        [in_vmem] * 4,
        (in_vmem,) * 3,
        [pltpu.SemaphoreType.DMA],
    )(near(ahead), near(with_ids), ids, scalars)
    cross2 = lax.ppermute(beside, AXES, two_along(size))

    far_specs = [in_vmem] * 5

    def far(image_if_even, own, other, total, loss):
        return call(
            functools.partial(far_kernel, image_if_even), (total_shape, loss_shape), far_specs, (in_vmem, in_vmem), aliases={3: 0, 4: 1}
        )(near(own), near(other), scalars, near(total), near(loss))

    ahead_total, beside_total, loss = call(
        near_kernel,
        (total_shape, total_shape, loss_shape),
        [in_vmem] * 7,
        (in_vmem,) * 3,
        aliases={6: 2},
    )(near(ahead), near(beside), near(chip1), near(own_slopes), ids, scalars, near(loss))

    cross1 = after(cross1, loss)
    cross3 = lax.ppermute(cross1, AXES, two_along(size))
    chip2 = lax.ppermute(cross1[:rows], AXES, swap_in_chip(size))
    ahead_total, loss = far(True, ahead, cross1, ahead_total, loss)
    chip3 = lax.ppermute(after(cross2, loss), AXES, swap_in_chip(size))
    beside_total, loss = far(False, beside, chip2, beside_total, loss)
    ahead_total, loss = far(True, ahead, cross2, ahead_total, loss)
    beside_grad, loss = call(
        beside_kernel,
        (block_shape, loss_shape),
        far_specs,
        (in_vmem, in_vmem),
        aliases={4: 1},
    )(near(beside), near(chip3), scalars, near(beside_total), near(loss))

    row_loss, grad_image, grad_text = call(
        ahead_kernel,
        (jax.ShapeDtypeStruct((1, rows), jnp.float32), grad_shape, grad_shape),
        far_specs + [in_vmem],
        (in_vmem, anywhere, anywhere),
        [pltpu.VMEM((rows, width), jnp.bfloat16), pltpu.SemaphoreType.DMA((3,))],
    )(near(ahead), near(cross3), scalars, near(ahead_total), near(loss), near(beside_grad))
    return row_loss.reshape(rows), grad_image, grad_text


def solution(mesh):
    in_specs = (P(AXES, None), P(AXES, None), P(AXES), P(), P())
    out_specs = (P(AXES), P(AXES, None), P(AXES, None))
    return jax.shard_map(local, mesh=mesh, in_specs=in_specs, out_specs=out_specs, check_vma=False)
```

time: 64.5 us -> 62.7 us (0.972)
  Pallas kernels: 21.9 us -> 20.7 us
  starting transfers between devices: 39.9 us -> 39.1 us
    pallas_call x4, Pallas kernels: 10.4 us -> 9.66 us  [the longest x1 4 us: local(): call(near_kernel, (total_shape, total_shape, loss_shape), [in_vmem] * 7,...]
  transfers between devices with their start and end apart: 6 -> 6, of which waited for: 0 -> 0; matrix products, arithmetic and copies ran while one was open for 0% -> 0% of each run, Pallas kernels for 27% -> 26%
where the time goes in v4:
time: 62.7 us; the launch traced here: 62.4 us
  starting transfers between devices  39.1 us (62%)
  Pallas kernels  20.7 us (33%)
  between operations  2.32 us (4%)
    ppermute x1, starting transfers between devices, local(): chip1 = lax.ppermute(with_ids, AXES, swap_in_chip(size))  14.3 us
    ppermute x1, starting transfers between devices, local(): cross3 = lax.ppermute(cross1, AXES, two_along(size))  12.7 us
    pallas_call x3, Pallas kernels, far(): call(functools.partial(far_kernel, image_if_even), (total_shape, loss_sha...  6.58 us
    ppermute x1, starting transfers between devices, local(): cross1 = lax.ppermute(ahead, AXES, swap_across(size))  4.59 us
    pallas_call x1, Pallas kernels, local(): call(near_kernel, (total_shape, total_shape, loss_shape), [in_vmem] * 7,...  4 us
    pallas_call x1, Pallas kernels, local(): call(ahead_kernel, (jax.ShapeDtypeStruct((1, rows), jnp.float32), grad_sh...  3.2 us
    ppermute x1, starting transfers between devices, local(): cross2 = lax.ppermute(beside, AXES, two_along(size))  2.97 us
    ppermute x1, starting transfers between devices, local(): chip3 = lax.ppermute(after(cross2, loss), AXES, swap_in_chip(size))  2.58 us
  transfers between devices with their start and end apart: 6, of which 0 were waited for; matrix products, arithmetic and copies ran while one was open for 0% of the time, Pallas kernels for 26%

profile of v4, /device:TPU:1, one launch (start us, length us, event | category | flops | bytes accessed | tf_op | source)
XLA Modules:
  0.0 62.4 jit_solution(8858504501844544497)
XLA Ops:
  0.6 0.0 copy-start
  0.6 1.3 %shard_map.79.ahead_ref.own_ref = bf16[528,1152]{1,0:T(8,128)(2,1)S(1)} custom-call(bf16[512,1152]{1,0:T(8,128)(2,1)} %odd_ref.2, bf16[512,1152]{1,0:T(8,128)(2,1)} %even_ref.3), custom_call_target="tpu_custom_call" | custom-call | flops 1 | bytes 1 | tf_op jit(solution)/shard_map/pallas_call | solution.py:284
  1.9 4.6 %collective-permute-start = (bf16[528,1152]{1,0:T(8,128)(2,1)S(1)}, bf16[528,1152]{1,0:T(8,128)(2,1)S(1)}, u32[]{:S(2)}, u32[]{:S(2)}) collective-permute-start(bf16[528,1152]{1,0:T(8,128)(2,1)S(1)} %shard_map.79.ahead_ref.own_ref), channel_id=1, source_target_pairs={{0,511},{1,2},{2,1},{3,4},{4,3},{5,6},{6,5},{7,8},{8,7},{9,10},{10... | collective-permute-start | bytes 3649544 | tf_op jit(solution)/shard_map/ppermute | solution.py:291
  6.5 0.0 copy-done
  6.5 1.3 %shard_map.80.with_ids_ref = bf16[528,1152]{1,0:T(8,128)(2,1)S(1)} custom-call(bf16[512,1152]{1,0:T(8,128)(2,1)} %even_ref.3, bf16[512,1152]{1,0:T(8,128)(2,1)} %odd_ref.2, s32[1,512]{1,0:T(1,128)S(1)} %bitcast.5), custom_call_target="tpu_custom_call" | custom-call | flops 1 | bytes 1 | tf_op jit(solution)/shard_map/pallas_call | solution.py:294
  7.8 14.3 %collective-permute-start.1 = (bf16[528,1152]{1,0:T(8,128)(2,1)S(1)}, bf16[528,1152]{1,0:T(8,128)(2,1)S(1)}, u32[]{:S(2)}, u32[]{:S(2)}) collective-permute-start(bf16[528,1152]{1,0:T(8,128)(2,1)S(1)} %shard_map.80.with_ids_ref), channel_id=1, source_target_pairs={{0,1},{1,0},{2,3},{3,2},{4,5},{5,4},{6,7},{7,6},{8,9},{9,8},{10,11... | collective-permute-start | bytes 3649544 | tf_op jit(solution)/shard_map/ppermute | solution.py:302
  23.5 0.1 iota.7.scalars_ref
  23.6 2.0 %shard_map.81 = (bf16[512,1152]{1,0:T(8,128)(2,1)S(1)}, bf16[512,512]{1,0:T(8,128)(2,1)S(1)}, f32[512,128]{1,0:T(8,128)S(1)}) custom-call(bf16[528,1152]{1,0:T(8,128)(2,1)S(1)} %shard_map.79.ahead_ref.own_ref, bf16[528,1152]{1,0:T(8,128)(2,1)S(1)} %shard_map.80.with_ids_ref, s32[1,512]{1,0:T(1,128)S(1)} %bitcast.6, f32[8,128]{1,0:T(8,128)S(1)} %iota.7.scalars_ref), custom_call_target="tpu_custom_call" | custom-call | flops 1 | bytes 1 | tf_op jit(solution)/shard_map/pallas_call | solution.py:304
  25.6 3.0 %collective-permute-start.3 = (bf16[512,1152]{1,0:T(8,128)(2,1)S(1)}, bf16[512,1152]{1,0:T(8,128)(2,1)S(1)}, u32[]{:S(2)}, u32[]{:S(2)}) collective-permute-start(bf16[512,1152]{1,0:T(8,128)(2,1)S(1)} %get-tuple-element.24.own_ref), channel_id=1, source_target_pairs={{0,2},{1,511},{2,4},{3,1},{4,6},{5,3},{6,8},{7,5},{8,10},{9,7},{10... | collective-permute-start | bytes 3538952 | tf_op jit(solution)/shard_map/ppermute | solution.py:311
  28.6 0.0 collective-permute-done.1.other_ref
  28.6 4.0 %shard_map.82 = (f32[512,1152]{1,0:T(8,128)S(1)}, f32[512,1152]{1,0:T(8,128)S(1)}, f32[512,128]{1,0:T(8,128)S(1)}) custom-call(bf16[528,1152]{1,0:T(8,128)(2,1)S(1)} %shard_map.79.ahead_ref.own_ref, bf16[512,1152]{1,0:T(8,128)(2,1)S(1)} %get-tuple-element.24.own_ref, ...), custom_call_target="tpu_custom_call", output_to_operand_aliasing={{2}: (6, {})} | custom-call | flops 1 | bytes 1 | tf_op jit(solution)/shard_map/pallas_call | solution.py:320
  32.6 0.0 collective-permute-done.other_ref
  32.6 12.7 %collective-permute-start.2 = (bf16[528,1152]{1,0:T(8,128)(2,1)S(1)}, bf16[528,1152]{1,0:T(8,128)(2,1)S(1)}, u32[]{:S(2)}, u32[]{:S(2)}) collective-permute-start(bf16[528,1152]{1,0:T(8,128)(2,1)S(1)} %collective-permute-done.other_ref), channel_id=1, source_target_pairs={{0,2},{1,511},{2,4},{3,1},{4,6},{5,3},{6,8},{7,5},{8,10},{9,7},{10... | collective-permute-start | bytes 3649544 | tf_op jit(solution)/shard_map/ppermute | solution.py:329
  45.4 0.1 slice.3
  45.5 1.9 %collective-permute-start.4 = (bf16[512,1152]{1,0:T(8,128)(2,1)S(1)}, bf16[512,1152]{1,0:T(8,128)(2,1)S(1)}, u32[]{:S(2)}, u32[]{:S(2)}) collective-permute-start(bf16[512,1152]{1,0:T(8,128)(2,1)S(1)} %slice.3), channel_id=1, source_target_pairs={{0,1},{1,0},{2,3},{3,2},{4,5},{5,4},{6,7},{7,6},{8,9},{9,8},{10,11... | collective-permute-start | bytes 3538952 | tf_op jit(solution)/shard_map/ppermute | solution.py:330
  47.4 2.3 %shard_map.83 = (f32[512,1152]{1,0:T(8,128)S(1)}, f32[512,128]{1,0:T(8,128)S(1)}) custom-call(bf16[528,1152]{1,0:T(8,128)(2,1)S(1)} %shard_map.79.ahead_ref.own_ref, bf16[528,1152]{1,0:T(8,128)(2,1)S(1)} %collective-permute-done.other_ref, f32[8,128]{1,0:T(8,128)S(1)} %iota.7.scalars_ref, ...), custom_call_target="tpu_custom_call", output_to_operand_aliasing={{0}: (3, {}), {1}: (4, {})} | custom-call | flops 1 | bytes 1 | tf_op jit(solution)/shard_map/pallas_call | solution.py:316
  49.7 0.0 collective-permute-done.3.other_ref
  49.7 2.6 %collective-permute-start.5 = (bf16[512,1152]{1,0:T(8,128)(2,1)S(1)}, bf16[512,1152]{1,0:T(8,128)(2,1)S(1)}, u32[]{:S(2)}, u32[]{:S(2)}) collective-permute-start(bf16[512,1152]{1,0:T(8,128)(2,1)S(1)} %collective-permute-done.3.other_ref), channel_id=1, source_target_pairs={{0,1},{1,0},{2,3},{3,2},{4,5},{5,4},{6,7},{7,6},{8,9},{9,8},{10,11... | collective-permute-start | bytes 3538952 | tf_op jit(solution)/shard_map/ppermute | solution.py:332
  52.3 0.0 collective-permute-done.4.other_ref
  52.3 2.2 %shard_map.84 = (f32[512,1152]{1,0:T(8,128)S(1)}, f32[512,128]{1,0:T(8,128)S(1)}) custom-call(bf16[512,1152]{1,0:T(8,128)(2,1)S(1)} %get-tuple-element.24.own_ref, bf16[512,1152]{1,0:T(8,128)(2,1)S(1)} %collective-permute-done.4.other_ref, f32[8,128]{1,0:T(8,128)S(1)} %iota.7.scalars_ref, ...), custom_call_target="tpu_custom_call", output_to_operand_aliasing={{0}: (3, {}), {1}: (4, {})} | custom-call | flops 1 | bytes 1 | tf_op jit(solution)/shard_map/pallas_call | solution.py:316
  54.5 2.1 %shard_map.85 = (f32[512,1152]{1,0:T(8,128)S(1)}, f32[512,128]{1,0:T(8,128)S(1)}) custom-call(bf16[528,1152]{1,0:T(8,128)(2,1)S(1)} %shard_map.79.ahead_ref.own_ref, bf16[512,1152]{1,0:T(8,128)(2,1)S(1)} %collective-permute-done.3.other_ref, f32[8,128]{1,0:T(8,128)S(1)} %iota.7.scalars_ref, ...), custom_call_target="tpu_custom_call", output_to_operand_aliasing={{0}: (3, {}), {1}: (4, {})} | custom-call | flops 1 | bytes 1 | tf_op jit(solution)/shard_map/pallas_call | solution.py:316
  56.6 0.0 collective-permute-done.5.other_ref
  56.6 2.3 %shard_map.86 = (bf16[512,1152]{1,0:T(8,128)(2,1)S(1)}, f32[512,128]{1,0:T(8,128)S(1)}) custom-call(bf16[512,1152]{1,0:T(8,128)(2,1)S(1)} %get-tuple-element.24.own_ref, bf16[512,1152]{1,0:T(8,128)(2,1)S(1)} %collective-permute-done.5.other_ref, f32[8,128]{1,0:T(8,128)S(1)} %iota.7.scalars_ref, ...), custom_call_target="tpu_custom_call", output_to_operand_aliasing={{1}: (4, {})} | custom-call | flops 1 | bytes 1 | tf_op jit(solution)/shard_map/pallas_call | solution.py:335
  59.0 0.0 collective-permute-done.2.other_ref
  59.0 3.2 %shard_map.87 = (f32[1,512]{1,0:T(1,128)}, bf16[512,1152]{1,0:T(8,128)(2,1)}, bf16[512,1152]{1,0:T(8,128)(2,1)}) custom-call(bf16[528,1152]{1,0:T(8,128)(2,1)S(1)} %shard_map.79.ahead_ref.own_ref, bf16[528,1152]{1,0:T(8,128)(2,1)S(1)} %collective-permute-done.2.other_ref, f32[8,128]{1,0:T(8,128)S(1)} %iota.7.scalars_ref, ...), custom_call_target="tpu_custom_call" | custom-call | flops 1 | bytes 1 | tf_op jit(solution)/shard_map/pallas_call | solution.py:343
  (1 shorter events, 0.0 us)
Async XLA Ops:
  0.6 5.9 %copy-start = (s32[512]{0:T(512)S(1)}, s32[512]{0:T(512)}, u32[]{:S(2)}) copy-start(s32[512]{0:T(512)} %param.7) | copy-start | bytes 6148
  1.9 30.7 %collective-permute-start = (bf16[528,1152]{1,0:T(8,128)(2,1)S(1)}, bf16[528,1152]{1,0:T(8,128)(2,1)S(1)}, u32[]{:S(2)}, u32[]{:S(2)}) collective-permute-start(bf16[528,1152]{1,0:T(8,128)(2,1)S(1)} %shard_map.79.ahead_ref.own_ref), channel_id=1, source_target_pairs={{0,511},{1,2},{2,1},{3,4},{4,3},{5,6},{6,5},{7,8},{8,7},{9,10},{10... | collective-permute-start | bytes 3649544 | tf_op jit(solution)/shard_map/ppermute | solution.py:291
  7.8 20.7 %collective-permute-start.1 = (bf16[528,1152]{1,0:T(8,128)(2,1)S(1)}, bf16[528,1152]{1,0:T(8,128)(2,1)S(1)}, u32[]{:S(2)}, u32[]{:S(2)}) collective-permute-start(bf16[528,1152]{1,0:T(8,128)(2,1)S(1)} %shard_map.80.with_ids_ref), channel_id=1, source_target_pairs={{0,1},{1,0},{2,3},{3,2},{4,5},{5,4},{6,7},{7,6},{8,9},{9,8},{10,11... | collective-permute-start | bytes 3649544 | tf_op jit(solution)/shard_map/ppermute | solution.py:302
  25.6 24.0 %collective-permute-start.3 = (bf16[512,1152]{1,0:T(8,128)(2,1)S(1)}, bf16[512,1152]{1,0:T(8,128)(2,1)S(1)}, u32[]{:S(2)}, u32[]{:S(2)}) collective-permute-start(bf16[512,1152]{1,0:T(8,128)(2,1)S(1)} %get-tuple-element.24.own_ref), channel_id=1, source_target_pairs={{0,2},{1,511},{2,4},{3,1},{4,6},{5,3},{6,8},{7,5},{8,10},{9,7},{10... | collective-permute-start | bytes 3538952 | tf_op jit(solution)/shard_map/ppermute | solution.py:311
  32.6 26.4 %collective-permute-start.2 = (bf16[528,1152]{1,0:T(8,128)(2,1)S(1)}, bf16[528,1152]{1,0:T(8,128)(2,1)S(1)}, u32[]{:S(2)}, u32[]{:S(2)}) collective-permute-start(bf16[528,1152]{1,0:T(8,128)(2,1)S(1)} %collective-permute-done.other_ref), channel_id=1, source_target_pairs={{0,2},{1,511},{2,4},{3,1},{4,6},{5,3},{6,8},{7,5},{8,10},{9,7},{10... | collective-permute-start | bytes 3649544 | tf_op jit(solution)/shard_map/ppermute | solution.py:329
  45.5 6.8 %collective-permute-start.4 = (bf16[512,1152]{1,0:T(8,128)(2,1)S(1)}, bf16[512,1152]{1,0:T(8,128)(2,1)S(1)}, u32[]{:S(2)}, u32[]{:S(2)}) collective-permute-start(bf16[512,1152]{1,0:T(8,128)(2,1)S(1)} %slice.3), channel_id=1, source_target_pairs={{0,1},{1,0},{2,3},{3,2},{4,5},{5,4},{6,7},{7,6},{8,9},{9,8},{10,11... | collective-permute-start | bytes 3538952 | tf_op jit(solution)/shard_map/ppermute | solution.py:330
  49.7 6.9 %collective-permute-start.5 = (bf16[512,1152]{1,0:T(8,128)(2,1)S(1)}, bf16[512,1152]{1,0:T(8,128)(2,1)S(1)}, u32[]{:S(2)}, u32[]{:S(2)}) collective-permute-start(bf16[512,1152]{1,0:T(8,128)(2,1)S(1)} %collective-permute-done.3.other_ref), channel_id=1, source_target_pairs={{0,1},{1,0},{2,3},{3,2},{4,5},{5,4},{6,7},{7,6},{8,9},{9,8},{10,11... | collective-permute-start | bytes 3538952 | tf_op jit(solution)/shard_map/ppermute | solution.py:332

commit v5 on v4

--- a/solution.py
+++ b/solution.py
@@ -218,7 +218,7 @@
     pair(own_ref, other_ref, scalars_ref, total_in, loss_in, loss_ref, False, store)
 
 
-def ahead_kernel(own_ref, other_ref, scalars_ref, total_in, loss_in, beside_ref, row_loss_ref, image_ref, text_ref, rounded_ref, sems):
+def ahead_kernel(own_ref, other_ref, scalars_ref, total_in, loss_in, beside_ref, row_loss_ref, image_ref, text_ref, rounded_ref, losses_ref, sems):
     scale, shift = scale_and_shift(scalars_ref)
     own_ref, other_ref = block_rows(own_ref, total_in), block_rows(other_ref, total_in)
     rows = total_in.shape[0]
@@ -231,22 +231,24 @@
         ahead_out, beside_out = (image_ref, text_ref) if even else (text_ref, image_ref)
         copies = [pltpu.make_async_copy(beside_ref, beside_out, sems.at[0])]
         copies[0].start()
-        logits = [scores(chunks[0])]
-        small = []
+        logits = scores(chunks[0])
         for at, chunk in enumerate(chunks):
-            small.append(jnp.exp(-jnp.abs(logits[at])))
-            slopes = slopes_of(logits[at], small[at])
-            if at + 1 < len(chunks):
-                logits.append(scores(chunks[at + 1]))
+            last = at + 1 == len(chunks)
+            small = jnp.exp(-jnp.abs(logits))
+            slopes = slopes_of(logits, small)
+            loss = loss_in[chunk, :]
+            if even:
+                loss = loss + fold(terms_of(logits, small))
+            losses_ref[:, chunk] = jnp.sum(loss.T, axis=0, keepdims=True) / (STEPS * rows)
+            if last:
+                copies.append(pltpu.make_async_copy(losses_ref, row_loss_ref, sems.at[at + 2]))
+                copies[-1].start()
+            else:
+                logits = scores(chunks[at + 1])
             total = total_in[chunk, :] + product(slopes, other_ref[...], 1, 0)
             rounded_ref[chunk, :] = (scale * total).astype(jnp.bfloat16)
             copies.append(pltpu.make_async_copy(rounded_ref.at[chunk, :], ahead_out.at[chunk, :], sems.at[at + 1]))
             copies[-1].start()
-        for at, chunk in enumerate(chunks):
-            loss = loss_in[chunk, :]
-            if even:
-                loss = loss + fold(terms_of(logits[at], small[at]))
-            row_loss_ref[:, chunk] = jnp.sum(loss.T, axis=0, keepdims=True) / (STEPS * rows)
         for copy in copies:
             copy.wait()
 
@@ -344,8 +346,8 @@
         ahead_kernel,
         (jax.ShapeDtypeStruct((1, rows), jnp.float32), grad_shape, grad_shape),
         far_specs + [in_vmem],
-        (in_vmem, anywhere, anywhere),
-        [pltpu.VMEM((rows, width), jnp.bfloat16), pltpu.SemaphoreType.DMA((3,))],
+        (anywhere, anywhere, anywhere),
+        [pltpu.VMEM((rows, width), jnp.bfloat16), pltpu.VMEM((1, rows), jnp.float32), pltpu.SemaphoreType.DMA((4,))],
     )(near(ahead), near(cross3), scalars, near(ahead_total), near(loss), near(beside_grad))
     return row_loss.reshape(rows), grad_image, grad_text
 

time: 62.7 us -> 62.1 us (level)
  no operation moved by 1% of the time
where the time goes in v5:
time: 62.1 us; the launch traced here: 61.8 us
  starting transfers between devices  39.1 us (63%)
  Pallas kernels  20.1 us (32%)
  between operations  2.32 us (4%)
    ppermute x1, starting transfers between devices, local(): chip1 = lax.ppermute(with_ids, AXES, swap_in_chip(size))  14.3 us
    ppermute x1, starting transfers between devices, local(): cross3 = lax.ppermute(cross1, AXES, two_along(size))  12.7 us
    pallas_call x3, Pallas kernels, far(): call(functools.partial(far_kernel, image_if_even), (total_shape, loss_sha...  6.58 us
    ppermute x1, starting transfers between devices, local(): cross1 = lax.ppermute(ahead, AXES, swap_across(size))  4.59 us
    pallas_call x1, Pallas kernels, local(): call(near_kernel, (total_shape, total_shape, loss_shape), [in_vmem] * 7,...  4 us
    ppermute x1, starting transfers between devices, local(): cross2 = lax.ppermute(beside, AXES, two_along(size))  2.97 us
    pallas_call x1, Pallas kernels, local(): call(ahead_kernel, (jax.ShapeDtypeStruct((1, rows), jnp.float32), grad_sh...  2.61 us
    ppermute x1, starting transfers between devices, local(): chip3 = lax.ppermute(after(cross2, loss), AXES, swap_in_chip(size))  2.58 us
  transfers between devices with their start and end apart: 6, of which 0 were waited for; matrix products, arithmetic and copies ran while one was open for 0% of the time, Pallas kernels for 26%

profile of v5, /device:TPU:1, one launch (start us, length us, event | category | flops | bytes accessed | tf_op | source)
XLA Modules:
  0.0 61.8 jit_solution(4175539433782910303)
XLA Ops:
  0.6 0.0 copy-start
  0.6 1.3 %shard_map.79.ahead_ref.own_ref = bf16[528,1152]{1,0:T(8,128)(2,1)S(1)} custom-call(bf16[512,1152]{1,0:T(8,128)(2,1)} %odd_ref.2, bf16[512,1152]{1,0:T(8,128)(2,1)} %even_ref.3), custom_call_target="tpu_custom_call" | custom-call | flops 1 | bytes 1 | tf_op jit(solution)/shard_map/pallas_call | solution.py:286
  1.9 4.6 %collective-permute-start = (bf16[528,1152]{1,0:T(8,128)(2,1)S(1)}, bf16[528,1152]{1,0:T(8,128)(2,1)S(1)}, u32[]{:S(2)}, u32[]{:S(2)}) collective-permute-start(bf16[528,1152]{1,0:T(8,128)(2,1)S(1)} %shard_map.79.ahead_ref.own_ref), channel_id=1, source_target_pairs={{0,511},{1,2},{2,1},{3,4},{4,3},{5,6},{6,5},{7,8},{8,7},{9,10},{10... | collective-permute-start | bytes 3649544 | tf_op jit(solution)/shard_map/ppermute | solution.py:293
  6.5 0.0 copy-done
  6.5 1.3 %shard_map.80.with_ids_ref = bf16[528,1152]{1,0:T(8,128)(2,1)S(1)} custom-call(bf16[512,1152]{1,0:T(8,128)(2,1)} %even_ref.3, bf16[512,1152]{1,0:T(8,128)(2,1)} %odd_ref.2, s32[1,512]{1,0:T(1,128)S(1)} %bitcast.5), custom_call_target="tpu_custom_call" | custom-call | flops 1 | bytes 1 | tf_op jit(solution)/shard_map/pallas_call | solution.py:296
  7.8 14.3 %collective-permute-start.1 = (bf16[528,1152]{1,0:T(8,128)(2,1)S(1)}, bf16[528,1152]{1,0:T(8,128)(2,1)S(1)}, u32[]{:S(2)}, u32[]{:S(2)}) collective-permute-start(bf16[528,1152]{1,0:T(8,128)(2,1)S(1)} %shard_map.80.with_ids_ref), channel_id=1, source_target_pairs={{0,1},{1,0},{2,3},{3,2},{4,5},{5,4},{6,7},{7,6},{8,9},{9,8},{10,11... | collective-permute-start | bytes 3649544 | tf_op jit(solution)/shard_map/ppermute | solution.py:304
  23.5 0.1 iota.7.scalars_ref
  23.6 2.0 %shard_map.81 = (bf16[512,1152]{1,0:T(8,128)(2,1)S(1)}, bf16[512,512]{1,0:T(8,128)(2,1)S(1)}, f32[512,128]{1,0:T(8,128)S(1)}) custom-call(bf16[528,1152]{1,0:T(8,128)(2,1)S(1)} %shard_map.79.ahead_ref.own_ref, bf16[528,1152]{1,0:T(8,128)(2,1)S(1)} %shard_map.80.with_ids_ref, s32[1,512]{1,0:T(1,128)S(1)} %bitcast.6, f32[8,128]{1,0:T(8,128)S(1)} %iota.7.scalars_ref), custom_call_target="tpu_custom_call" | custom-call | flops 1 | bytes 1 | tf_op jit(solution)/shard_map/pallas_call | solution.py:306
  25.6 3.0 %collective-permute-start.3 = (bf16[512,1152]{1,0:T(8,128)(2,1)S(1)}, bf16[512,1152]{1,0:T(8,128)(2,1)S(1)}, u32[]{:S(2)}, u32[]{:S(2)}) collective-permute-start(bf16[512,1152]{1,0:T(8,128)(2,1)S(1)} %get-tuple-element.24.own_ref), channel_id=1, source_target_pairs={{0,2},{1,511},{2,4},{3,1},{4,6},{5,3},{6,8},{7,5},{8,10},{9,7},{10... | collective-permute-start | bytes 3538952 | tf_op jit(solution)/shard_map/ppermute | solution.py:313
  28.6 0.0 collective-permute-done.1.other_ref
  28.6 4.0 %shard_map.82 = (f32[512,1152]{1,0:T(8,128)S(1)}, f32[512,1152]{1,0:T(8,128)S(1)}, f32[512,128]{1,0:T(8,128)S(1)}) custom-call(bf16[528,1152]{1,0:T(8,128)(2,1)S(1)} %shard_map.79.ahead_ref.own_ref, bf16[512,1152]{1,0:T(8,128)(2,1)S(1)} %get-tuple-element.24.own_ref, ...), custom_call_target="tpu_custom_call", output_to_operand_aliasing={{2}: (6, {})} | custom-call | flops 1 | bytes 1 | tf_op jit(solution)/shard_map/pallas_call | solution.py:322
  32.6 0.0 collective-permute-done.other_ref
  32.6 12.7 %collective-permute-start.2 = (bf16[528,1152]{1,0:T(8,128)(2,1)S(1)}, bf16[528,1152]{1,0:T(8,128)(2,1)S(1)}, u32[]{:S(2)}, u32[]{:S(2)}) collective-permute-start(bf16[528,1152]{1,0:T(8,128)(2,1)S(1)} %collective-permute-done.other_ref), channel_id=1, source_target_pairs={{0,2},{1,511},{2,4},{3,1},{4,6},{5,3},{6,8},{7,5},{8,10},{9,7},{10... | collective-permute-start | bytes 3649544 | tf_op jit(solution)/shard_map/ppermute | solution.py:331
  45.4 0.1 slice.3
  45.5 1.9 %collective-permute-start.4 = (bf16[512,1152]{1,0:T(8,128)(2,1)S(1)}, bf16[512,1152]{1,0:T(8,128)(2,1)S(1)}, u32[]{:S(2)}, u32[]{:S(2)}) collective-permute-start(bf16[512,1152]{1,0:T(8,128)(2,1)S(1)} %slice.3), channel_id=1, source_target_pairs={{0,1},{1,0},{2,3},{3,2},{4,5},{5,4},{6,7},{7,6},{8,9},{9,8},{10,11... | collective-permute-start | bytes 3538952 | tf_op jit(solution)/shard_map/ppermute | solution.py:332
  47.4 2.3 %shard_map.83 = (f32[512,1152]{1,0:T(8,128)S(1)}, f32[512,128]{1,0:T(8,128)S(1)}) custom-call(bf16[528,1152]{1,0:T(8,128)(2,1)S(1)} %shard_map.79.ahead_ref.own_ref, bf16[528,1152]{1,0:T(8,128)(2,1)S(1)} %collective-permute-done.other_ref, f32[8,128]{1,0:T(8,128)S(1)} %iota.7.scalars_ref, ...), custom_call_target="tpu_custom_call", output_to_operand_aliasing={{0}: (3, {}), {1}: (4, {})} | custom-call | flops 1 | bytes 1 | tf_op jit(solution)/shard_map/pallas_call | solution.py:318
  49.7 0.0 collective-permute-done.3.other_ref
  49.7 2.6 %collective-permute-start.5 = (bf16[512,1152]{1,0:T(8,128)(2,1)S(1)}, bf16[512,1152]{1,0:T(8,128)(2,1)S(1)}, u32[]{:S(2)}, u32[]{:S(2)}) collective-permute-start(bf16[512,1152]{1,0:T(8,128)(2,1)S(1)} %collective-permute-done.3.other_ref), channel_id=1, source_target_pairs={{0,1},{1,0},{2,3},{3,2},{4,5},{5,4},{6,7},{7,6},{8,9},{9,8},{10,11... | collective-permute-start | bytes 3538952 | tf_op jit(solution)/shard_map/ppermute | solution.py:334
  52.3 0.0 collective-permute-done.4.other_ref
  52.3 2.2 %shard_map.84 = (f32[512,1152]{1,0:T(8,128)S(1)}, f32[512,128]{1,0:T(8,128)S(1)}) custom-call(bf16[512,1152]{1,0:T(8,128)(2,1)S(1)} %get-tuple-element.24.own_ref, bf16[512,1152]{1,0:T(8,128)(2,1)S(1)} %collective-permute-done.4.other_ref, f32[8,128]{1,0:T(8,128)S(1)} %iota.7.scalars_ref, ...), custom_call_target="tpu_custom_call", output_to_operand_aliasing={{0}: (3, {}), {1}: (4, {})} | custom-call | flops 1 | bytes 1 | tf_op jit(solution)/shard_map/pallas_call | solution.py:318
  54.5 2.1 %shard_map.85 = (f32[512,1152]{1,0:T(8,128)S(1)}, f32[512,128]{1,0:T(8,128)S(1)}) custom-call(bf16[528,1152]{1,0:T(8,128)(2,1)S(1)} %shard_map.79.ahead_ref.own_ref, bf16[512,1152]{1,0:T(8,128)(2,1)S(1)} %collective-permute-done.3.other_ref, f32[8,128]{1,0:T(8,128)S(1)} %iota.7.scalars_ref, ...), custom_call_target="tpu_custom_call", output_to_operand_aliasing={{0}: (3, {}), {1}: (4, {})} | custom-call | flops 1 | bytes 1 | tf_op jit(solution)/shard_map/pallas_call | solution.py:318
  56.6 0.0 collective-permute-done.5.other_ref
  56.6 2.3 %shard_map.86 = (bf16[512,1152]{1,0:T(8,128)(2,1)S(1)}, f32[512,128]{1,0:T(8,128)S(1)}) custom-call(bf16[512,1152]{1,0:T(8,128)(2,1)S(1)} %get-tuple-element.24.own_ref, bf16[512,1152]{1,0:T(8,128)(2,1)S(1)} %collective-permute-done.5.other_ref, f32[8,128]{1,0:T(8,128)S(1)} %iota.7.scalars_ref, ...), custom_call_target="tpu_custom_call", output_to_operand_aliasing={{1}: (4, {})} | custom-call | flops 1 | bytes 1 | tf_op jit(solution)/shard_map/pallas_call | solution.py:337
  59.0 0.0 collective-permute-done.2.other_ref
  59.0 2.6 %shard_map.87 = (f32[1,512]{1,0:T(1,128)}, bf16[512,1152]{1,0:T(8,128)(2,1)}, bf16[512,1152]{1,0:T(8,128)(2,1)}) custom-call(bf16[528,1152]{1,0:T(8,128)(2,1)S(1)} %shard_map.79.ahead_ref.own_ref, bf16[528,1152]{1,0:T(8,128)(2,1)S(1)} %collective-permute-done.2.other_ref, f32[8,128]{1,0:T(8,128)S(1)} %iota.7.scalars_ref, ...), custom_call_target="tpu_custom_call" | custom-call | flops 1 | bytes 1 | tf_op jit(solution)/shard_map/pallas_call | solution.py:345
  (1 shorter events, 0.0 us)
Async XLA Ops:
  0.6 5.9 %copy-start = (s32[512]{0:T(512)S(1)}, s32[512]{0:T(512)}, u32[]{:S(2)}) copy-start(s32[512]{0:T(512)} %param.7) | copy-start | bytes 6148
  1.9 30.7 %collective-permute-start = (bf16[528,1152]{1,0:T(8,128)(2,1)S(1)}, bf16[528,1152]{1,0:T(8,128)(2,1)S(1)}, u32[]{:S(2)}, u32[]{:S(2)}) collective-permute-start(bf16[528,1152]{1,0:T(8,128)(2,1)S(1)} %shard_map.79.ahead_ref.own_ref), channel_id=1, source_target_pairs={{0,511},{1,2},{2,1},{3,4},{4,3},{5,6},{6,5},{7,8},{8,7},{9,10},{10... | collective-permute-start | bytes 3649544 | tf_op jit(solution)/shard_map/ppermute | solution.py:293
  7.8 20.7 %collective-permute-start.1 = (bf16[528,1152]{1,0:T(8,128)(2,1)S(1)}, bf16[528,1152]{1,0:T(8,128)(2,1)S(1)}, u32[]{:S(2)}, u32[]{:S(2)}) collective-permute-start(bf16[528,1152]{1,0:T(8,128)(2,1)S(1)} %shard_map.80.with_ids_ref), channel_id=1, source_target_pairs={{0,1},{1,0},{2,3},{3,2},{4,5},{5,4},{6,7},{7,6},{8,9},{9,8},{10,11... | collective-permute-start | bytes 3649544 | tf_op jit(solution)/shard_map/ppermute | solution.py:304
  25.6 24.0 %collective-permute-start.3 = (bf16[512,1152]{1,0:T(8,128)(2,1)S(1)}, bf16[512,1152]{1,0:T(8,128)(2,1)S(1)}, u32[]{:S(2)}, u32[]{:S(2)}) collective-permute-start(bf16[512,1152]{1,0:T(8,128)(2,1)S(1)} %get-tuple-element.24.own_ref), channel_id=1, source_target_pairs={{0,2},{1,511},{2,4},{3,1},{4,6},{5,3},{6,8},{7,5},{8,10},{9,7},{10... | collective-permute-start | bytes 3538952 | tf_op jit(solution)/shard_map/ppermute | solution.py:313
  32.6 26.4 %collective-permute-start.2 = (bf16[528,1152]{1,0:T(8,128)(2,1)S(1)}, bf16[528,1152]{1,0:T(8,128)(2,1)S(1)}, u32[]{:S(2)}, u32[]{:S(2)}) collective-permute-start(bf16[528,1152]{1,0:T(8,128)(2,1)S(1)} %collective-permute-done.other_ref), channel_id=1, source_target_pairs={{0,2},{1,511},{2,4},{3,1},{4,6},{5,3},{6,8},{7,5},{8,10},{9,7},{10... | collective-permute-start | bytes 3649544 | tf_op jit(solution)/shard_map/ppermute | solution.py:331
  45.5 6.8 %collective-permute-start.4 = (bf16[512,1152]{1,0:T(8,128)(2,1)S(1)}, bf16[512,1152]{1,0:T(8,128)(2,1)S(1)}, u32[]{:S(2)}, u32[]{:S(2)}) collective-permute-start(bf16[512,1152]{1,0:T(8,128)(2,1)S(1)} %slice.3), channel_id=1, source_target_pairs={{0,1},{1,0},{2,3},{3,2},{4,5},{5,4},{6,7},{7,6},{8,9},{9,8},{10,11... | collective-permute-start | bytes 3538952 | tf_op jit(solution)/shard_map/ppermute | solution.py:332
  49.7 6.9 %collective-permute-start.5 = (bf16[512,1152]{1,0:T(8,128)(2,1)S(1)}, bf16[512,1152]{1,0:T(8,128)(2,1)S(1)}, u32[]{:S(2)}, u32[]{:S(2)}) collective-permute-start(bf16[512,1152]{1,0:T(8,128)(2,1)S(1)} %collective-permute-done.3.other_ref), channel_id=1, source_target_pairs={{0,1},{1,0},{2,3},{3,2},{4,5},{5,4},{6,7},{7,6},{8,9},{9,8},{10,11... | collective-permute-start | bytes 3538952 | tf_op jit(solution)/shard_map/ppermute | solution.py:334

commit v6 on v5

--- a/solution.py
+++ b/solution.py
@@ -11,6 +11,7 @@
 DIGITS = 3
 AXES = ("rows", "cols")
 LANES = 128
+RUN = 16
 SPARE = 16
 VMEM_LIMIT = 24 * 1024 * 1024
 
@@ -138,24 +139,55 @@
     return ref.at[: like.shape[0], :]
 
 
-def own_kernel(ahead_ref, with_ids_ref, ids_ref, scalars_ref, beside_ref, slopes_ref, loss_ref, sem):
-    beside_copy = pltpu.make_async_copy(block_rows(with_ids_ref, beside_ref), beside_ref, sem)
-    beside_copy.start()
-    scale, shift = scale_and_shift(scalars_ref)
-    ids = ids_ref[...]
-    down = ids_down(ids)
-    ahead_ref, with_ids_ref = block_rows(ahead_ref, beside_ref), block_rows(with_ids_ref, beside_ref)
-
+def on_some(where, body):
+    if where is None:
+        body()
+        return
+    places, among = where
+    at = lax.rem(lax.axis_index("cols"), RUN)
+    here = functools.reduce(jnp.logical_or, [at == place for place in places])
+    pl.when(here if among else jnp.logical_not(here))(body)
+
+
+def own_scores(where, ahead_ref, beside_ref, ids_ref, scalars_ref, slopes_ref, loss_ref):
     def body(even):
-        image_ref, text_ref = (ahead_ref, with_ids_ref) if even else (with_ids_ref, ahead_ref)
+        scale, shift = scale_and_shift(scalars_ref)
+        ids = ids_ref[...]
+        down = ids_down(ids)
+        image_ref, text_ref = (ahead_ref, beside_ref) if even else (beside_ref, ahead_ref)
         for chunk in halves(image_ref.shape[0]):
             logits = scale * product(image_ref[chunk, :], text_ref[...], 1, 1) + shift
             small, positive = jnp.exp(-jnp.abs(logits)), match(down[chunk, :], ids)
             slopes_ref[chunk, :] = slopes_of(logits, small, positive)
             loss_ref[chunk, :] = fold(terms_of(logits, small, positive))
 
-    by_parity(True, body)
+    on_some(where, lambda: by_parity(True, body))
+
+
+def own_products(where, ahead_ref, beside_ref, slopes_ref, ahead_total, beside_total):
+    def body(even):
+        image_ref, text_ref = (ahead_ref, beside_ref) if even else (beside_ref, ahead_ref)
+        image_total, text_total = (ahead_total, beside_total) if even else (beside_total, ahead_total)
+        image_total[...] = product(slopes_ref[...], text_ref[...], 1, 0)
+        text_total[...] = product(slopes_ref[...], image_ref[...], 0, 0)
+
+    on_some(where, lambda: by_parity(True, body))
+
+
+def own_kernel(ahead_ref, with_ids_ref, ids_ref, scalars_ref, beside_ref, slopes_ref, loss_ref, sem):
+    beside_copy = pltpu.make_async_copy(block_rows(with_ids_ref, beside_ref), beside_ref, sem)
+    beside_copy.start()
+    ahead_ref, with_ids_ref = block_rows(ahead_ref, beside_ref), block_rows(with_ids_ref, beside_ref)
+    own_scores(((0,), False), ahead_ref, with_ids_ref, ids_ref, scalars_ref, slopes_ref, loss_ref)
     beside_copy.wait()
+
+
+def later_scores_kernel(ahead_ref, beside_ref, ids_ref, scalars_ref, slopes_in, loss_in, slopes_ref, loss_ref):
+    own_scores(((0,), True), block_rows(ahead_ref, beside_ref), beside_ref, ids_ref, scalars_ref, slopes_ref, loss_ref)
+
+
+def early_products_kernel(ahead_ref, beside_ref, slopes_ref, ahead_total, beside_total):
+    own_products(((1, RUN - 1), True), block_rows(ahead_ref, beside_ref), beside_ref, slopes_ref, ahead_total, beside_total)
 
 
 def pair(own_ref, other_ref, scalars_ref, total_in, loss_in, loss_ref, image_if_even, store, ids=None):
@@ -191,22 +223,14 @@
     return store
 
 
-def near_kernel(ahead_ref, own_ref, other_ref, own_slopes_ref, ids_ref, scalars_ref, loss_in, ahead_total, total_ref, loss_ref):
-    ahead_ref = block_rows(ahead_ref, own_ref)
-
-    def body(even):
-        image_ref, text_ref = (ahead_ref, own_ref) if even else (own_ref, ahead_ref)
-        image_total, text_total = (ahead_total, total_ref) if even else (total_ref, ahead_total)
-        image_total[...] = product(own_slopes_ref[...], text_ref[...], 1, 0)
-        text_total[...] = product(own_slopes_ref[...], image_ref[...], 0, 0)
-
-    by_parity(True, body)
+def near_kernel(ahead_ref, own_ref, other_ref, own_slopes_ref, ids_ref, scalars_ref, ahead_in, total_in, loss_in, ahead_total, total_ref, loss_ref):
+    own_products(((1, RUN - 1), False), block_rows(ahead_ref, own_ref), own_ref, own_slopes_ref, ahead_total, total_ref)
     ids = (ids_ref[...], read_ids(other_ref, own_ref.shape[0]))
     pair(own_ref, other_ref, scalars_ref, total_ref, loss_in, loss_ref, False, keep(total_ref), ids)
 
 
-def far_kernel(image_if_even, own_ref, other_ref, scalars_ref, total_in, loss_in, total_ref, loss_ref):
-    pair(own_ref, other_ref, scalars_ref, total_in, loss_in, loss_ref, image_if_even, keep(total_ref))
+def far_kernel(image_if_even, where, own_ref, other_ref, scalars_ref, total_in, loss_in, total_ref, loss_ref):
+    on_some(where, lambda: pair(own_ref, other_ref, scalars_ref, total_in, loss_in, loss_ref, image_if_even, keep(total_ref)))
 
 
 def beside_kernel(own_ref, other_ref, scalars_ref, total_in, loss_in, rounded_ref, loss_ref):
@@ -279,6 +303,7 @@
     anywhere = pl.BlockSpec(memory_space=pl.ANY)
     total_shape = pltpu.VMEM((rows, width), jnp.float32)
     loss_shape = pltpu.VMEM((rows, LANES), jnp.float32)
+    slopes_shape = pltpu.VMEM((rows, rows), jnp.bfloat16)
     block_shape = pltpu.VMEM((rows, width), jnp.bfloat16)
     grad_shape = jax.ShapeDtypeStruct((rows, width), jnp.bfloat16)
     in_hbm = lambda array: pltpu.with_memory_space_constraint(array, pltpu.HBM)
@@ -305,32 +330,46 @@
 
     beside, own_slopes, loss = call(
         own_kernel,
-        (block_shape, pltpu.VMEM((rows, rows), jnp.bfloat16), loss_shape),
+        (block_shape, slopes_shape, loss_shape),
         [in_vmem] * 4,
         (in_vmem,) * 3,
         [pltpu.SemaphoreType.DMA],
     )(near(ahead), near(with_ids), ids, scalars)
-    cross2 = lax.ppermute(beside, AXES, two_along(size))
+    ahead_total, beside_total = call(
+        early_products_kernel,
+        (total_shape, total_shape),
+        [in_vmem] * 3,
+        (in_vmem,) * 2,
+    )(near(ahead), near(beside), near(own_slopes))
+    cross2 = lax.ppermute(after(beside, ahead_total), AXES, two_along(size))
+    own_slopes, loss = call(
+        later_scores_kernel,
+        (slopes_shape, loss_shape),
+        [in_vmem] * 6,
+        (in_vmem,) * 2,
+        aliases={4: 0, 5: 1},
+    )(near(ahead), near(beside), ids, scalars, near(own_slopes), near(loss))
 
     far_specs = [in_vmem] * 5
 
-    def far(image_if_even, own, other, total, loss):
+    def far(image_if_even, own, other, total, loss, where=None):
         return call(
-            functools.partial(far_kernel, image_if_even), (total_shape, loss_shape), far_specs, (in_vmem, in_vmem), aliases={3: 0, 4: 1}
+            functools.partial(far_kernel, image_if_even, where), (total_shape, loss_shape), far_specs, (in_vmem, in_vmem), aliases={3: 0, 4: 1}
         )(near(own), near(other), scalars, near(total), near(loss))
 
     ahead_total, beside_total, loss = call(
         near_kernel,
         (total_shape, total_shape, loss_shape),
-        [in_vmem] * 7,
+        [in_vmem] * 9,
         (in_vmem,) * 3,
-        aliases={6: 2},
-    )(near(ahead), near(beside), near(chip1), near(own_slopes), ids, scalars, near(loss))
+        aliases={6: 0, 7: 1, 8: 2},
+    )(near(ahead), near(beside), near(chip1), near(own_slopes), ids, scalars, near(ahead_total), near(beside_total), near(loss))
 
     cross1 = after(cross1, loss)
-    cross3 = lax.ppermute(cross1, AXES, two_along(size))
-    chip2 = lax.ppermute(cross1[:rows], AXES, swap_in_chip(size))
-    ahead_total, loss = far(True, ahead, cross1, ahead_total, loss)
+    ahead_total, loss = far(True, ahead, cross1, ahead_total, loss, ((1,), True))
+    cross3 = lax.ppermute(after(cross1, loss), AXES, two_along(size))
+    ahead_total, loss = far(True, ahead, cross1, ahead_total, loss, ((1,), False))
+    chip2 = lax.ppermute(after(cross1, loss)[:rows], AXES, swap_in_chip(size))
     chip3 = lax.ppermute(after(cross2, loss), AXES, swap_in_chip(size))
     beside_total, loss = far(False, beside, chip2, beside_total, loss)
     ahead_total, loss = far(True, ahead, cross2, ahead_total, loss)

time: 62.1 us -> 61.4 us (0.989)
  starting transfers between devices: 39.1 us -> 36.2 us
  waiting for transfers between devices: 0.02 us -> 2.28 us
    ppermute x3, starting transfers between devices: 17.6 us -> 14 us  [the longest x1 9.1 us: local(): cross3 = lax.ppermute(after(cross1, loss), AXES, two_along(size))]
    ppermute x3, waiting for transfers between devices: 0.01 us -> 2.27 us  [the longest x1 2.27 us: local(): cross3 = lax.ppermute(after(cross1, loss), AXES, two_along(size))]
    ppermute x1, starting transfers between devices: 2.58 us -> 3.33 us  [local(): chip3 = lax.ppermute(after(cross2, loss), AXES, swap_in_chip(size))]
    pallas_call x5 -> x8, Pallas kernels: 12.6 us -> 12.8 us  [the longest x4 6.66 us: far(): call(functools.partial(far_kernel, image_if_even, where), (total_shape, l...]
  transfers between devices with their start and end apart: 6 -> 6, of which waited for: 0 -> 1; matrix products, arithmetic and copies ran while one was open for 0% -> 0% of each run, Pallas kernels for 26% -> 26%
where the time goes in v6:
time: 61.4 us; the launch traced here: 61.1 us
  starting transfers between devices  36.2 us (59%)
  Pallas kernels  20.1 us (33%)
  between operations  2.33 us (4%)
  waiting for transfers between devices  2.28 us (4%)
    ppermute x1, starting transfers between devices, local(): chip1 = lax.ppermute(with_ids, AXES, swap_in_chip(size))  14.3 us
    ppermute x1, starting transfers between devices, local(): cross3 = lax.ppermute(after(cross1, loss), AXES, two_along(size))  9.1 us
    pallas_call x4, Pallas kernels, far(): call(functools.partial(far_kernel, image_if_even, where), (total_shape, l...  6.66 us
    ppermute x1, starting transfers between devices, local(): cross1 = lax.ppermute(ahead, AXES, swap_across(size))  4.59 us
    ppermute x1, starting transfers between devices, local(): chip3 = lax.ppermute(after(cross2, loss), AXES, swap_in_chip(size))  3.33 us
    ppermute x1, starting transfers between devices, local(): cross2 = lax.ppermute(after(beside, ahead_total), AXES, two_along(size))  2.98 us
    pallas_call x1, Pallas kernels, local(): call(near_kernel, (total_shape, total_shape, loss_shape), [in_vmem] * 9,...  2.63 us
    pallas_call x1, Pallas kernels, local(): call(ahead_kernel, (jax.ShapeDtypeStruct((1, rows), jnp.float32), grad_sh...  2.59 us
  transfers between devices with their start and end apart: 6, of which 1 were waited for; matrix products, arithmetic and copies ran while one was open for 0% of the time, Pallas kernels for 26%

profile of v6, /device:TPU:1, one launch (start us, length us, event | category | flops | bytes accessed | tf_op | source)
XLA Modules:
  0.0 61.1 jit_solution(6080466422615172947)
XLA Ops:
  0.6 0.0 copy-start
  0.6 1.3 %shard_map.79.ahead_ref.own_ref = bf16[528,1152]{1,0:T(8,128)(2,1)S(1)} custom-call(bf16[512,1152]{1,0:T(8,128)(2,1)} %odd_ref.2, bf16[512,1152]{1,0:T(8,128)(2,1)} %even_ref.3), custom_call_target="tpu_custom_call" | custom-call | flops 1 | bytes 1 | tf_op jit(solution)/shard_map/pallas_call | solution.py:311
  1.9 4.6 %collective-permute-start = (bf16[528,1152]{1,0:T(8,128)(2,1)S(1)}, bf16[528,1152]{1,0:T(8,128)(2,1)S(1)}, u32[]{:S(2)}, u32[]{:S(2)}) collective-permute-start(bf16[528,1152]{1,0:T(8,128)(2,1)S(1)} %shard_map.79.ahead_ref.own_ref), channel_id=1, source_target_pairs={{0,511},{1,2},{2,1},{3,4},{4,3},{5,6},{6,5},{7,8},{8,7},{9,10},{10... | collective-permute-start | bytes 3649544 | tf_op jit(solution)/shard_map/ppermute | solution.py:318
  6.5 0.0 copy-done
  6.5 1.3 %shard_map.80.with_ids_ref = bf16[528,1152]{1,0:T(8,128)(2,1)S(1)} custom-call(bf16[512,1152]{1,0:T(8,128)(2,1)} %even_ref.3, bf16[512,1152]{1,0:T(8,128)(2,1)} %odd_ref.2, s32[1,512]{1,0:T(1,128)S(1)} %bitcast.5), custom_call_target="tpu_custom_call" | custom-call | flops 1 | bytes 1 | tf_op jit(solution)/shard_map/pallas_call | solution.py:321
  7.8 14.3 %collective-permute-start.1 = (bf16[528,1152]{1,0:T(8,128)(2,1)S(1)}, bf16[528,1152]{1,0:T(8,128)(2,1)S(1)}, u32[]{:S(2)}, u32[]{:S(2)}) collective-permute-start(bf16[528,1152]{1,0:T(8,128)(2,1)S(1)} %shard_map.80.with_ids_ref), channel_id=1, source_target_pairs={{0,1},{1,0},{2,3},{3,2},{4,5},{5,4},{6,7},{7,6},{8,9},{9,8},{10,11... | collective-permute-start | bytes 3649544 | tf_op jit(solution)/shard_map/ppermute | solution.py:329
  23.5 0.1 iota.7.scalars_ref
  23.6 1.9 %shard_map.81 = (bf16[512,1152]{1,0:T(8,128)(2,1)S(1)}, bf16[512,512]{1,0:T(8,128)(2,1)S(1)}, f32[512,128]{1,0:T(8,128)S(1)}) custom-call(bf16[528,1152]{1,0:T(8,128)(2,1)S(1)} %shard_map.79.ahead_ref.own_ref, bf16[528,1152]{1,0:T(8,128)(2,1)S(1)} %shard_map.80.with_ids_ref, s32[1,512]{1,0:T(1,128)S(1)} %bitcast.6, f32[8,128]{1,0:T(8,128)S(1)} %iota.7.scalars_ref), custom_call_target="tpu_custom_call" | custom-call | flops 1 | bytes 1 | tf_op jit(solution)/shard_map/pallas_call | solution.py:331
  25.5 1.6 %shard_map.83 = (f32[512,1152]{1,0:T(8,128)S(1)}, f32[512,1152]{1,0:T(8,128)S(1)}) custom-call(bf16[528,1152]{1,0:T(8,128)(2,1)S(1)} %shard_map.79.ahead_ref.own_ref, bf16[512,1152]{1,0:T(8,128)(2,1)S(1)} %get-tuple-element.45.beside_ref.own_ref, bf16[512,512]{1,0:T(8,128)(2,1)S(1)} %get-tuple-element.34.slopes_in.slopes_ref), custom_call_target="tpu_custom_call" | custom-call | flops 1 | bytes 1 | tf_op jit(solution)/shard_map/pallas_call | solution.py:338
  27.1 3.0 %collective-permute-start.3 = (bf16[512,1152]{1,0:T(8,128)(2,1)S(1)}, bf16[512,1152]{1,0:T(8,128)(2,1)S(1)}, u32[]{:S(2)}, u32[]{:S(2)}) collective-permute-start(bf16[512,1152]{1,0:T(8,128)(2,1)S(1)} %get-tuple-element.45.beside_ref.own_ref), channel_id=1, source_target_pairs={{0,2},{1,511},{2,4},{3,1},{4,6},{5,3},{6,8},{7,5},{8,10},{9,7},{10... | collective-permute-start | bytes 3538952 | tf_op jit(solution)/shard_map/ppermute | solution.py:344
  30.1 0.0 collective-permute-done.1.other_ref
  30.1 2.6 %shard_map.84 = (f32[512,1152]{1,0:T(8,128)S(1)}, f32[512,1152]{1,0:T(8,128)S(1)}, f32[512,128]{1,0:T(8,128)S(1)}) custom-call(bf16[528,1152]{1,0:T(8,128)(2,1)S(1)} %shard_map.79.ahead_ref.own_ref, bf16[512,1152]{1,0:T(8,128)(2,1)S(1)} %get-tuple-element.45.beside_ref.own_ref, ...), custom_call_target="tpu_custom_call", output_to_operand_aliasing={{0}: (6, {}), {1}: (7, {}), {2}: (8, {})} | custom-call | flops 1 | bytes 1 | tf_op jit(solution)/shard_map/pallas_call | solution.py:360
  32.7 0.0 collective-permute-done.other_ref
  32.7 2.1 %shard_map.85 = (f32[512,1152]{1,0:T(8,128)S(1)}, f32[512,128]{1,0:T(8,128)S(1)}) custom-call(bf16[528,1152]{1,0:T(8,128)(2,1)S(1)} %shard_map.79.ahead_ref.own_ref, bf16[528,1152]{1,0:T(8,128)(2,1)S(1)} %collective-permute-done.other_ref, f32[8,128]{1,0:T(8,128)S(1)} %iota.7.scalars_ref, ...), custom_call_target="tpu_custom_call", output_to_operand_aliasing={{0}: (3, {}), {1}: (4, {})} | custom-call | flops 1 | bytes 1 | tf_op jit(solution)/shard_map/pallas_call | solution.py:356
  34.8 9.1 %collective-permute-start.2 = (bf16[528,1152]{1,0:T(8,128)(2,1)S(1)}, bf16[528,1152]{1,0:T(8,128)(2,1)S(1)}, u32[]{:S(2)}, u32[]{:S(2)}) collective-permute-start(bf16[528,1152]{1,0:T(8,128)(2,1)S(1)} %collective-permute-done.other_ref), channel_id=1, source_target_pairs={{0,2},{1,511},{2,4},{3,1},{4,6},{5,3},{6,8},{7,5},{8,10},{9,7},{10... | collective-permute-start | bytes 3649544 | tf_op jit(solution)/shard_map/ppermute | solution.py:370
  43.9 0.1 slice.3
  44.0 1.9 %collective-permute-start.4 = (bf16[512,1152]{1,0:T(8,128)(2,1)S(1)}, bf16[512,1152]{1,0:T(8,128)(2,1)S(1)}, u32[]{:S(2)}, u32[]{:S(2)}) collective-permute-start(bf16[512,1152]{1,0:T(8,128)(2,1)S(1)} %slice.3), channel_id=1, source_target_pairs={{0,1},{1,0},{2,3},{3,2},{4,5},{5,4},{6,7},{7,6},{8,9},{9,8},{10,11... | collective-permute-start | bytes 3538952 | tf_op jit(solution)/shard_map/ppermute | solution.py:372
  46.0 0.0 collective-permute-done.3.other_ref
  46.0 3.3 %collective-permute-start.5 = (bf16[512,1152]{1,0:T(8,128)(2,1)S(1)}, bf16[512,1152]{1,0:T(8,128)(2,1)S(1)}, u32[]{:S(2)}, u32[]{:S(2)}) collective-permute-start(bf16[512,1152]{1,0:T(8,128)(2,1)S(1)} %collective-permute-done.3.other_ref), channel_id=1, source_target_pairs={{0,1},{1,0},{2,3},{3,2},{4,5},{5,4},{6,7},{7,6},{8,9},{9,8},{10,11... | collective-permute-start | bytes 3538952 | tf_op jit(solution)/shard_map/ppermute | solution.py:373
  49.3 0.0 collective-permute-done.4.other_ref
  49.3 2.5 %shard_map.87 = (f32[512,1152]{1,0:T(8,128)S(1)}, f32[512,128]{1,0:T(8,128)S(1)}) custom-call(bf16[512,1152]{1,0:T(8,128)(2,1)S(1)} %get-tuple-element.45.beside_ref.own_ref, bf16[512,1152]{1,0:T(8,128)(2,1)S(1)} %collective-permute-done.4.other_ref, f32[8,128]{1,0:T(8,128)S(1)} %iota.7.scalars_ref, ...), custom_call_target="tpu_custom_call", output_to_operand_aliasing={{0}: (3, {}), {1}: (4, {})} | custom-call | flops 1 | bytes 1 | tf_op jit(solution)/shard_map/pallas_call | solution.py:356
  51.8 2.1 %shard_map.88 = (f32[512,1152]{1,0:T(8,128)S(1)}, f32[512,128]{1,0:T(8,128)S(1)}) custom-call(bf16[528,1152]{1,0:T(8,128)(2,1)S(1)} %shard_map.79.ahead_ref.own_ref, bf16[512,1152]{1,0:T(8,128)(2,1)S(1)} %collective-permute-done.3.other_ref, f32[8,128]{1,0:T(8,128)S(1)} %iota.7.scalars_ref, ...), custom_call_target="tpu_custom_call", output_to_operand_aliasing={{0}: (3, {}), {1}: (4, {})} | custom-call | flops 1 | bytes 1 | tf_op jit(solution)/shard_map/pallas_call | solution.py:356
  53.9 0.0 collective-permute-done.5.other_ref
  53.9 2.1 %shard_map.89 = (bf16[512,1152]{1,0:T(8,128)(2,1)S(1)}, f32[512,128]{1,0:T(8,128)S(1)}) custom-call(bf16[512,1152]{1,0:T(8,128)(2,1)S(1)} %get-tuple-element.45.beside_ref.own_ref, bf16[512,1152]{1,0:T(8,128)(2,1)S(1)} %collective-permute-done.5.other_ref, f32[8,128]{1,0:T(8,128)S(1)} %iota.7.scalars_ref, ...), custom_call_target="tpu_custom_call", output_to_operand_aliasing={{1}: (4, {})} | custom-call | flops 1 | bytes 1 | tf_op jit(solution)/shard_map/pallas_call | solution.py:376
  56.0 2.3 %collective-permute-done.2.other_ref = bf16[528,1152]{1,0:T(8,128)(2,1)S(1)} collective-permute-done((bf16[528,1152]{1,0:T(8,128)(2,1)S(1)}, bf16[528,1152]{1,0:T(8,128)(2,1)S(1)}, u32[]{:S(2)}, u32[]{:S(2)}) %collective-permute-start.2) | collective-permute-done | bytes 1216544 | tf_op jit(solution)/shard_map/ppermute | solution.py:370
  58.3 2.6 %shard_map.90 = (f32[1,512]{1,0:T(1,128)}, bf16[512,1152]{1,0:T(8,128)(2,1)}, bf16[512,1152]{1,0:T(8,128)(2,1)}) custom-call(bf16[528,1152]{1,0:T(8,128)(2,1)S(1)} %shard_map.79.ahead_ref.own_ref, bf16[528,1152]{1,0:T(8,128)(2,1)S(1)} %collective-permute-done.2.other_ref, f32[8,128]{1,0:T(8,128)S(1)} %iota.7.scalars_ref, ...), custom_call_target="tpu_custom_call" | custom-call | flops 1 | bytes 1 | tf_op jit(solution)/shard_map/pallas_call | solution.py:384
  (3 shorter events, 0.0 us)
Async XLA Ops:
  0.6 5.9 %copy-start = (s32[512]{0:T(512)S(1)}, s32[512]{0:T(512)}, u32[]{:S(2)}) copy-start(s32[512]{0:T(512)} %param.7) | copy-start | bytes 6148
  1.9 30.8 %collective-permute-start = (bf16[528,1152]{1,0:T(8,128)(2,1)S(1)}, bf16[528,1152]{1,0:T(8,128)(2,1)S(1)}, u32[]{:S(2)}, u32[]{:S(2)}) collective-permute-start(bf16[528,1152]{1,0:T(8,128)(2,1)S(1)} %shard_map.79.ahead_ref.own_ref), channel_id=1, source_target_pairs={{0,511},{1,2},{2,1},{3,4},{4,3},{5,6},{6,5},{7,8},{8,7},{9,10},{10... | collective-permute-start | bytes 3649544 | tf_op jit(solution)/shard_map/ppermute | solution.py:318
  7.8 22.2 %collective-permute-start.1 = (bf16[528,1152]{1,0:T(8,128)(2,1)S(1)}, bf16[528,1152]{1,0:T(8,128)(2,1)S(1)}, u32[]{:S(2)}, u32[]{:S(2)}) collective-permute-start(bf16[528,1152]{1,0:T(8,128)(2,1)S(1)} %shard_map.80.with_ids_ref), channel_id=1, source_target_pairs={{0,1},{1,0},{2,3},{3,2},{4,5},{5,4},{6,7},{7,6},{8,9},{9,8},{10,11... | collective-permute-start | bytes 3649544 | tf_op jit(solution)/shard_map/ppermute | solution.py:329
  27.1 18.9 %collective-permute-start.3 = (bf16[512,1152]{1,0:T(8,128)(2,1)S(1)}, bf16[512,1152]{1,0:T(8,128)(2,1)S(1)}, u32[]{:S(2)}, u32[]{:S(2)}) collective-permute-start(bf16[512,1152]{1,0:T(8,128)(2,1)S(1)} %get-tuple-element.45.beside_ref.own_ref), channel_id=1, source_target_pairs={{0,2},{1,511},{2,4},{3,1},{4,6},{5,3},{6,8},{7,5},{8,10},{9,7},{10... | collective-permute-start | bytes 3538952 | tf_op jit(solution)/shard_map/ppermute | solution.py:344
  34.8 23.5 %collective-permute-start.2 = (bf16[528,1152]{1,0:T(8,128)(2,1)S(1)}, bf16[528,1152]{1,0:T(8,128)(2,1)S(1)}, u32[]{:S(2)}, u32[]{:S(2)}) collective-permute-start(bf16[528,1152]{1,0:T(8,128)(2,1)S(1)} %collective-permute-done.other_ref), channel_id=1, source_target_pairs={{0,2},{1,511},{2,4},{3,1},{4,6},{5,3},{6,8},{7,5},{8,10},{9,7},{10... | collective-permute-start | bytes 3649544 | tf_op jit(solution)/shard_map/ppermute | solution.py:370
  44.0 5.3 %collective-permute-start.4 = (bf16[512,1152]{1,0:T(8,128)(2,1)S(1)}, bf16[512,1152]{1,0:T(8,128)(2,1)S(1)}, u32[]{:S(2)}, u32[]{:S(2)}) collective-permute-start(bf16[512,1152]{1,0:T(8,128)(2,1)S(1)} %slice.3), channel_id=1, source_target_pairs={{0,1},{1,0},{2,3},{3,2},{4,5},{5,4},{6,7},{7,6},{8,9},{9,8},{10,11... | collective-permute-start | bytes 3538952 | tf_op jit(solution)/shard_map/ppermute | solution.py:372
  46.0 7.9 %collective-permute-start.5 = (bf16[512,1152]{1,0:T(8,128)(2,1)S(1)}, bf16[512,1152]{1,0:T(8,128)(2,1)S(1)}, u32[]{:S(2)}, u32[]{:S(2)}) collective-permute-start(bf16[512,1152]{1,0:T(8,128)(2,1)S(1)} %collective-permute-done.3.other_ref), channel_id=1, source_target_pairs={{0,1},{1,0},{2,3},{3,2},{4,5},{5,4},{6,7},{7,6},{8,9},{9,8},{10,11... | collective-permute-start | bytes 3538952 | tf_op jit(solution)/shard_map/ppermute | solution.py:373
